TPU v7x, 128 devices: a whole 4x4x4 slice. The times are simulated.
128 devices in a mesh: wide: 32 (over y, z, x_hi), narrow: 4 (over x_lo, core).
Axes of the slice: x: 4 (x_hi: 2, x_lo: 2; x = x_hi * 2 + x_lo), y: 4, z: 4, core: 2. Of those that a mesh axis runs over, the one named last changes fastest.
Arguments:
- hidden_in: bfloat16 [2, 8192, 768], P(None, ('wide', 'narrow')), may hold values from -6 to 6
- lengths: int32 [2], replicated, may hold values from 2048 to 8192, as said below
- w_qkv: bfloat16 [768, 2304], P('wide', 'narrow'), may hold values from -0.3125 to 0.3125
- w_out: bfloat16 [768, 768], P('wide', 'narrow'), may hold values from -1.75 to 1.75
- w_gate: bfloat16 [768, 3072], P('wide', 'narrow'), may hold values from -0.21875 to 0.21875
- w_up: bfloat16 [768, 3072], P('wide', 'narrow'), may hold values from -0.21875 to 0.21875
- w_down: bfloat16 [3072, 768], P('wide', 'narrow'), may hold values from -0.21875 to 0.21875
- norm_params: bfloat16 [4, 768], P('narrow', 'wide'), may hold values from 0.5 to 1.5
- cotangent: bfloat16 [2, 8192, 768], P(None, ('wide', 'narrow')), may hold values from -6 to 6
Outputs:
- layer_out: bfloat16 [2, 8192, 768], P(None, ('wide', 'narrow'))
- grad_input: bfloat16 [2, 8192, 768], P(None, ('wide', 'narrow'))
- grad_qkv: float32 [768, 2304], P('wide', 'narrow')
- grad_out: float32 [768, 768], P('wide', 'narrow')
- grad_gate: float32 [768, 3072], P('wide', 'narrow')
- grad_up: float32 [768, 3072], P('wide', 'narrow')
- grad_down: float32 [3072, 768], P('wide', 'narrow')
- grad_norms: float32 [4, 768], P('narrow', 'wide')
Inputs may be any that keep to these rules, and one draw needn't show every extreme that they name: Each sequence's valid tokens are the first lengths[s] of its 8192 slots; in every draw one sequence has all 8192 valid.
All inputs are finite; a program needn't handle non-finite values.
Results may differ from a plain program's by a relative error of at most 0.035.
Values may be sent and summed in bfloat16 or wider, within the bound.
No kernel may reach another device: no remote copies, remote signals or barrier semaphores. Data moves between devices by JAX's collectives and lax.ppermute only.
A program may use at most 192 MiB of HBM per device.

v0:
```python
import jax
import jax.numpy as jnp
from jax import lax
from jax.sharding import PartitionSpec as P

HEADS = 12
HEAD = 64


EPSILON = 1e-05


def rope_tables(positions, head_size):
    freqs = 10000.0 ** (-2.0 * jnp.arange(head_size // 2, dtype=jnp.float32) / head_size)
    angles = positions.astype(jnp.float32)[:, None] * freqs[None, :]
    cosine_table = jnp.cos(angles)
    sine_table = jnp.sin(angles)
    cosine_full = jnp.concatenate([cosine_table, cosine_table], -1)
    sine_full = jnp.concatenate([sine_table, sine_table], -1)
    return (cosine_full[None, :, None, :], sine_full[None, :, None, :])


def rotate(values, cosine_table, sine_table):
    half_width = values.shape[-1] // 2
    turned = jnp.concatenate([-values[..., half_width:], values[..., :half_width]], -1)
    return values * cosine_table + turned * sine_table


def unrotate(incoming, cosine_table, sine_table):
    half_width = incoming.shape[-1] // 2
    scaled = incoming * sine_table
    return incoming * cosine_table + jnp.concatenate(
        [scaled[..., half_width:], -scaled[..., :half_width]], -1
    )


def layer_norm_parts(residual, gain_vec, bias_vec):
    row_mean = jnp.mean(residual, -1, keepdims=True)
    centred = residual - row_mean
    variance = jnp.mean(centred * centred, -1, keepdims=True)
    inv_std = lax.rsqrt(variance + EPSILON)
    unit_rows = centred * inv_std
    return (unit_rows * gain_vec + bias_vec, unit_rows, inv_std)


def norm_back(incoming, unit_rows, inv_std, gain_vec):
    scaled = incoming * gain_vec
    return inv_std * (
        scaled
        - jnp.mean(scaled, -1, keepdims=True)
        - unit_rows * jnp.mean(scaled * unit_rows, -1, keepdims=True)
    )


def over_keys(step_fn, carried, pieces):
    piece_rows = pieces[0].shape[1]
    sub_rows = 1024
    sub_count = piece_rows // sub_rows

    def one_turn(carry_in, sub_index):
        parts = tuple(
            (
                lax.dynamic_slice_in_dim(member, sub_index * sub_rows, sub_rows, 1)
                for member in pieces
            )
        )
        return (step_fn(carry_in, parts, sub_index * sub_rows), None)

    carried, _ = lax.scan(one_turn, carried, jnp.arange(sub_count))
    return carried


def on_device(hidden_in, lengths, w_qkv, w_out, w_gate, w_up, w_down, norm_params, cotangent):
    narrow_n = lax.axis_size("narrow")
    wide_i = lax.axis_index("wide")
    narrow_i = lax.axis_index("narrow")
    seq_count, slot_count, model_width = hidden_in.shape
    heads_here = HEADS // narrow_n
    local_width = model_width // narrow_n
    group_slots = slot_count * narrow_n
    score_scale = HEAD ** (-0.5)
    f32 = jnp.float32
    bf16 = jnp.bfloat16
    part_qkv, part_out, part_gate, part_up, part_down, part_norms = (
        lax.all_gather(w_qkv, "narrow", axis=1, tiled=True),
        lax.all_gather(w_out, "narrow", axis=1, tiled=True),
        lax.all_gather(w_gate, "narrow", axis=1, tiled=True),
        lax.all_gather(w_up, "narrow", axis=1, tiled=True),
        lax.all_gather(w_down, "narrow", axis=1, tiled=True),
        lax.all_gather(norm_params, "narrow", axis=0, tiled=True),
    )
    wqkv, wout, wgate, wup, wdown, norms_full = (
        lax.all_gather(part_qkv, "wide", axis=0, tiled=True),
        lax.all_gather(part_out, "wide", axis=0, tiled=True),
        lax.all_gather(part_gate, "wide", axis=0, tiled=True),
        lax.all_gather(part_up, "wide", axis=0, tiled=True),
        lax.all_gather(part_down, "wide", axis=0, tiled=True),
        lax.all_gather(part_norms, "wide", axis=1, tiled=True),
    )
    norm_values = norms_full.astype(f32)
    mine_start = (wide_i * narrow_n + narrow_i) * slot_count
    positions = mine_start + jnp.arange(slot_count)
    valid_rows = (positions[None, :] < lengths[:, None]).astype(f32)
    mask_flat = valid_rows.reshape(-1, 1)
    token_rows = hidden_in.reshape(-1, model_width)
    projected = jnp.dot(token_rows, wqkv, preferred_element_type=f32).reshape(
        seq_count, slot_count, 3 * model_width
    )
    cosine_mine, sine_mine = rope_tables(positions, HEAD)
    query_rot = rotate(
        projected[..., :model_width].reshape(seq_count, slot_count, HEADS, HEAD),
        cosine_mine,
        sine_mine,
    )
    key_rot = rotate(
        projected[..., model_width : 2 * model_width].reshape(seq_count, slot_count, HEADS, HEAD),
        cosine_mine,
        sine_mine,
    )
    stacked = jnp.stack(
        [
            query_rot.reshape(seq_count, slot_count, model_width),
            key_rot.reshape(seq_count, slot_count, model_width),
            projected[..., 2 * model_width :],
        ],
        axis=2,
    ).astype(bf16)
    regrouped_in = lax.all_to_all(stacked, "narrow", split_axis=3, concat_axis=1, tiled=True)
    query_flat = regrouped_in[:, :, 0]
    key_flat = regrouped_in[:, :, 1]
    value_flat = regrouped_in[:, :, 2]
    query_here = query_flat.reshape(seq_count, group_slots, heads_here, HEAD)
    key_here = key_flat.reshape(seq_count, group_slots, heads_here, HEAD)
    value_here = value_flat.reshape(seq_count, group_slots, heads_here, HEAD)
    block_start = wide_i * group_slots
    block_positions = block_start + jnp.arange(group_slots)
    my_key_mask = (block_positions[None, :] < lengths[:, None])[:, None, None, :]

    def forward_step(carried, pieces, first_row):
        running_max, running_sum, weighted = carried
        key_part, value_part = pieces
        piece_rows = key_part.shape[1]
        key_part = key_part.reshape(seq_count, piece_rows, heads_here, HEAD)
        value_part = value_part.reshape(seq_count, piece_rows, heads_here, HEAD)
        key_mask = ((first_row + jnp.arange(piece_rows))[None, :] < lengths[:, None])[
            :, None, None, :
        ]
        scores = (
            jnp.einsum("sqhd,skhd->shqk", query_here, key_part, preferred_element_type=f32)
            * score_scale
        )
        scores = jnp.where(key_mask, scores, -1e30)
        new_max = jnp.maximum(running_max, jnp.max(scores, -1))
        probs = jnp.where(key_mask, jnp.exp(scores - new_max[..., None]), 0.0)
        factor = jnp.exp(running_max - new_max)
        running_sum = running_sum * factor + jnp.sum(probs, -1)
        weighted = weighted * jnp.transpose(factor, (0, 2, 1))[..., None] + jnp.einsum(
            "shqk,skhd->sqhd", probs.astype(bf16), value_part, preferred_element_type=f32
        )
        return (new_max, running_sum, weighted)

    start_state = (
        jnp.full((seq_count, heads_here, group_slots), -1e30, f32),
        jnp.zeros((seq_count, heads_here, group_slots), f32),
        jnp.zeros((seq_count, group_slots, heads_here, HEAD), f32),
    )
    running_max, running_sum, weighted = over_keys(
        forward_step,
        start_state,
        (
            lax.all_gather(key_flat, "wide", axis=1, tiled=True),
            lax.all_gather(value_flat, "wide", axis=1, tiled=True),
        ),
    )
    log_sum = running_max + jnp.log(running_sum)
    attended = weighted / jnp.transpose(running_sum, (0, 2, 1))[..., None]
    attn_sent = attended.reshape(seq_count, group_slots, local_width).astype(bf16)
    regrouped = lax.all_to_all(
        attn_sent, "narrow", split_axis=1, concat_axis=2, tiled=True
    ).reshape(-1, model_width)
    projection = jnp.dot(regrouped, wout, preferred_element_type=f32)
    normed, unit_first, inv_first = layer_norm_parts(
        token_rows.astype(f32) + projection, norm_values[0], norm_values[1]
    )
    normed_low = normed.astype(bf16)
    gate_pre = jnp.dot(normed_low, wgate, preferred_element_type=f32)
    up_pre = jnp.dot(normed_low, wup, preferred_element_type=f32)
    gate_sigmoid = jax.nn.sigmoid(gate_pre)
    gate_silu = gate_pre * gate_sigmoid
    activated = (gate_silu * up_pre).astype(bf16)
    down_out = jnp.dot(activated, wdown, preferred_element_type=f32)
    output_rows, unit_second, inv_second = layer_norm_parts(
        normed + down_out, norm_values[2], norm_values[3]
    )
    layer_out = (output_rows * mask_flat).astype(bf16).reshape(seq_count, slot_count, model_width)
    grad_rows = cotangent.reshape(-1, model_width).astype(f32) * mask_flat
    grad_gain2 = jnp.sum(grad_rows * unit_second, 0)
    grad_bias2 = jnp.sum(grad_rows, 0)
    grad_second = norm_back(grad_rows, unit_second, inv_second, norm_values[2])
    grad_down_low = grad_second.astype(bf16)
    grad_wdown = jnp.einsum("tf,td->fd", activated, grad_down_low, preferred_element_type=f32)
    grad_act = jnp.einsum("td,fd->tf", grad_down_low, wdown, preferred_element_type=f32)
    silu_slope = gate_sigmoid * (1.0 + gate_pre * (1.0 - gate_sigmoid))
    grad_gate_low = (grad_act * up_pre * silu_slope).astype(bf16)
    grad_up_low = (grad_act * gate_silu).astype(bf16)
    grad_wgate = jnp.einsum("td,tf->df", normed_low, grad_gate_low, preferred_element_type=f32)
    grad_wup = jnp.einsum("td,tf->df", normed_low, grad_up_low, preferred_element_type=f32)
    grad_normed = (
        grad_second
        + jnp.einsum("tf,df->td", grad_gate_low, wgate, preferred_element_type=f32)
        + jnp.einsum("tf,df->td", grad_up_low, wup, preferred_element_type=f32)
    )
    grad_gain1 = jnp.sum(grad_normed * unit_first, 0)
    grad_bias1 = jnp.sum(grad_normed, 0)
    grad_first = norm_back(grad_normed, unit_first, inv_first, norm_values[0])
    grad_proj_low = grad_first.astype(bf16)
    grad_wout = jnp.einsum("td,te->de", regrouped, grad_proj_low, preferred_element_type=f32)
    grad_attn = jnp.einsum("te,de->td", grad_proj_low, wout, preferred_element_type=f32).astype(
        bf16
    )
    grad_heads = lax.all_to_all(
        grad_attn.reshape(seq_count, slot_count, model_width),
        "narrow",
        split_axis=2,
        concat_axis=1,
        tiled=True,
    )
    grad_here = grad_heads.reshape(seq_count, group_slots, heads_here, HEAD)
    row_delta = jnp.transpose(jnp.sum(grad_here.astype(f32) * attended, -1), (0, 2, 1))
    all_lse, all_delta = (
        lax.all_gather(log_sum, "wide", axis=2, tiled=True),
        lax.all_gather(row_delta, "wide", axis=2, tiled=True),
    )

    def query_step(carried, pieces, first_row):
        key_part, value_part = pieces
        piece_rows = key_part.shape[1]
        key_part = key_part.reshape(seq_count, piece_rows, heads_here, HEAD)
        value_part = value_part.reshape(seq_count, piece_rows, heads_here, HEAD)
        key_mask = ((first_row + jnp.arange(piece_rows))[None, :] < lengths[:, None])[
            :, None, None, :
        ]
        scores = (
            jnp.einsum("sqhd,skhd->shqk", query_here, key_part, preferred_element_type=f32)
            * score_scale
        )
        probs = jnp.where(key_mask, jnp.exp(scores - log_sum[..., None]), 0.0)
        grad_probs = jnp.einsum(
            "sqhd,skhd->shqk", grad_here, value_part, preferred_element_type=f32
        )
        grad_scores = (probs * (grad_probs - row_delta[..., None])).astype(bf16)
        return (
            carried
            + jnp.einsum("shqk,skhd->sqhd", grad_scores, key_part, preferred_element_type=f32)
            * score_scale
        )

    grad_query = over_keys(
        query_step,
        jnp.zeros((seq_count, group_slots, heads_here, HEAD), f32),
        (
            lax.all_gather(key_flat, "wide", axis=1, tiled=True),
            lax.all_gather(value_flat, "wide", axis=1, tiled=True),
        ),
    )

    def key_step(carried, pieces, first_row):
        grad_key, grad_value = carried
        query_part, grad_part = pieces
        piece_rows = query_part.shape[1]
        query_part = query_part.reshape(seq_count, piece_rows, heads_here, HEAD)
        grad_part = grad_part.reshape(seq_count, piece_rows, heads_here, HEAD)
        lse_part = lax.dynamic_slice_in_dim(all_lse, first_row, piece_rows, 2)
        delta_part = lax.dynamic_slice_in_dim(all_delta, first_row, piece_rows, 2)
        scores = (
            jnp.einsum("sqhd,skhd->shqk", query_part, key_here, preferred_element_type=f32)
            * score_scale
        )
        probs = jnp.where(my_key_mask, jnp.exp(scores - lse_part[..., None]), 0.0)
        grad_probs = jnp.einsum(
            "sqhd,skhd->shqk", grad_part, value_here, preferred_element_type=f32
        )
        grad_scores = (probs * (grad_probs - delta_part[..., None])).astype(bf16)
        grad_key = (
            grad_key
            + jnp.einsum("shqk,sqhd->skhd", grad_scores, query_part, preferred_element_type=f32)
            * score_scale
        )
        grad_value = grad_value + jnp.einsum(
            "shqk,sqhd->skhd", probs.astype(bf16), grad_part, preferred_element_type=f32
        )
        return (grad_key, grad_value)

    zero_keys = jnp.zeros((seq_count, group_slots, heads_here, HEAD), f32)
    grad_key, grad_value = over_keys(
        key_step,
        (zero_keys, zero_keys),
        (
            lax.all_gather(query_flat, "wide", axis=1, tiled=True),
            lax.all_gather(grad_heads, "wide", axis=1, tiled=True),
        ),
    )
    cosine_block, sine_block = rope_tables(block_positions, HEAD)
    stacked_grads = jnp.stack(
        [
            unrotate(grad_query, cosine_block, sine_block).reshape(
                seq_count, group_slots, local_width
            ),
            unrotate(grad_key, cosine_block, sine_block).reshape(
                seq_count, group_slots, local_width
            ),
            grad_value.reshape(seq_count, group_slots, local_width),
        ],
        axis=2,
    ).astype(bf16)
    grad_projected = lax.all_to_all(
        stacked_grads, "narrow", split_axis=1, concat_axis=3, tiled=True
    ).reshape(-1, 3 * model_width)
    grad_wqkv = jnp.einsum("td,te->de", token_rows, grad_projected, preferred_element_type=f32)
    grad_input = grad_first + jnp.einsum(
        "te,de->td", grad_projected, wqkv, preferred_element_type=f32
    )
    grad_input = grad_input.astype(bf16).reshape(seq_count, slot_count, model_width)
    grad_norm_rows = jnp.stack([grad_gain1, grad_bias1, grad_gain2, grad_bias2])
    sum_qkv, sum_out, sum_gate, sum_up, sum_down, sum_norms = (
        lax.psum_scatter(
            grad_wqkv.astype(jnp.bfloat16), "wide", scatter_dimension=0, tiled=True
        ).astype(jnp.float32),
        lax.psum_scatter(
            grad_wout.astype(jnp.bfloat16), "wide", scatter_dimension=0, tiled=True
        ).astype(jnp.float32),
        lax.psum_scatter(
            grad_wgate.astype(jnp.bfloat16), "wide", scatter_dimension=0, tiled=True
        ).astype(jnp.float32),
        lax.psum_scatter(
            grad_wup.astype(jnp.bfloat16), "wide", scatter_dimension=0, tiled=True
        ).astype(jnp.float32),
        lax.psum_scatter(
            grad_wdown.astype(jnp.bfloat16), "wide", scatter_dimension=0, tiled=True
        ).astype(jnp.float32),
        lax.psum_scatter(
            grad_norm_rows.astype(jnp.bfloat16), "wide", scatter_dimension=1, tiled=True
        ).astype(jnp.float32),
    )
    sum_qkv, sum_out, sum_gate, sum_up, sum_down, sum_norms = (
        lax.psum_scatter(
            sum_qkv.astype(jnp.bfloat16), "narrow", scatter_dimension=1, tiled=True
        ).astype(jnp.float32),
        lax.psum_scatter(
            sum_out.astype(jnp.bfloat16), "narrow", scatter_dimension=1, tiled=True
        ).astype(jnp.float32),
        lax.psum_scatter(
            sum_gate.astype(jnp.bfloat16), "narrow", scatter_dimension=1, tiled=True
        ).astype(jnp.float32),
        lax.psum_scatter(
            sum_up.astype(jnp.bfloat16), "narrow", scatter_dimension=1, tiled=True
        ).astype(jnp.float32),
        lax.psum_scatter(
            sum_down.astype(jnp.bfloat16), "narrow", scatter_dimension=1, tiled=True
        ).astype(jnp.float32),
        lax.psum_scatter(
            sum_norms.astype(jnp.bfloat16), "narrow", scatter_dimension=0, tiled=True
        ).astype(jnp.float32),
    )
    return (layer_out, grad_input, sum_qkv, sum_out, sum_gate, sum_up, sum_down, sum_norms)


def solution(mesh):
    placed = (
        P(None, ("wide", "narrow"), None),
        P(),
        P("wide", "narrow"),
        P("wide", "narrow"),
        P("wide", "narrow"),
        P("wide", "narrow"),
        P("wide", "narrow"),
        P("narrow", "wide"),
        P(None, ("wide", "narrow"), None),
    )
    return jax.shard_map(
        on_device,
        mesh=mesh,
        in_specs=placed,
        out_specs=(
            P(None, ("wide", "narrow"), None),
            P(None, ("wide", "narrow"), None),
            P("wide", "narrow"),
            P("wide", "narrow"),
            P("wide", "narrow"),
            P("wide", "narrow"),
            P("wide", "narrow"),
            P("narrow", "wide"),
        ),
        check_vma=False,
    )
```

profile of v0, /device:TPU:1, one launch (start us, length us, event | category | flops | bytes accessed | tf_op | source)
XLA Modules:
  0.0 2118.9 jit_solution(6201904844186799217)
XLA Ops:
  7.2 6.9 all-gather.3
  16.8 76.5 %all-gather.17.cloned.1.call-done = bf16[768,2304]{1,0:T(8,128)(2,1)} async-done(((bf16[24,2304]{1,0:T(8,128)(2,1)}), bf16[768,2304]{1,0:T(8,128)(2,1)}) %all-gather.17.cloned.1.call-update) | async-done | bytes 3538960 | tf_op jit(solution)/shard_map/all_gather | solution.py:93
  101.9 13.0 all_to_all.66
  118.3 5.8 all-gather.4
  124.9 6.0 all_gather.64
  131.0 6.0 all_gather.66
  137.1 5.6 all_gather.68
  143.6 5.0 all-gather.5
  148.6 78.8 %all-gather.6 = bf16[32,24,4]{1,2,0:T(4,128)(2,1)S(1)} all-gather(bf16[1,24,4]{1,2,0:T(4,128)(2,1)S(1)} %bitcast.292), channel_id=1, replica_groups=mesh['wide'=32,'narrow'=4] {'wide'}, dimensions={0}, use_global_device_ids=true | all-gather | bytes 6336 | tf_op jit(solution)/shard_map/all_gather | solution.py:98
  229.5 10.2 copy.132
  239.7 86.0 %all-gather.31.cloned.1.call-done = bf16[2,8192,1,192]{3,1,2,0:T(8,128)(2,1)} async-done(((bf16[2,256,1,192]{3,1,2,0:T(8,128)(2,1)}), bf16[2,8192,1,192]{3,1,2,0:T(8,128)(2,1)}) %all-gather.31.cloned.1.call-update) | async-done | bytes 6291472 | tf_op jit(solution)/shard_map/all_gather | solution.py:172
  325.7 10.1 copy.133
  335.8 103.1 %while.39 = (s32[]{:T(128)}, f32[2,3,256]{2,1,0:T(4,128)S(1)}, f32[2,3,256]{2,1,0:T(4,128)S(1)}, f32[2,256,3,64]{1,3,2,0:T(8,128)S(1)}, s32[8]{0:T(128)S(1)}, /*...) while((s32[]{:T(128)}, f32[2,3,256]{2,1,0:T(4,128)S(1)}, ...), condition=%wide.region_3.4_spmd.clone, body=%wide.region_0.3_spmd.clone.sunk | while | flops 423407616 | bytes 49856748 | solution.py:69
  393.6 4.3 fusion.153
  439.8 4.4 all-to-all-start.1
  444.5 4.9 all-to-all-done.1
  451.9 26.3 %all-gather.21.cloned.1.call-done = bf16[768,3072]{1,0:T(8,128)(2,1)} async-done(((bf16[24,3072]{1,0:T(8,128)(2,1)}), bf16[768,3072]{1,0:T(8,128)(2,1)}) %all-gather.21.cloned.1.call-update) | async-done | bytes 4718608 | tf_op jit(solution)/shard_map/all_gather | solution.py:95
  482.5 80.5 %all-gather.23.cloned.1.call-done = bf16[768,3072]{1,0:T(8,128)(2,1)} async-done(((bf16[24,3072]{1,0:T(8,128)(2,1)}), bf16[768,3072]{1,0:T(8,128)(2,1)}) %all-gather.23.cloned.1.call-update) | async-done | bytes 4718608 | tf_op jit(solution)/shard_map/all_gather | solution.py:96
  563.0 5.0 multiply_convert_fusion.18
  568.1 80.5 %all-gather.25.cloned.1.call-done = bf16[3072,768]{1,0:T(8,128)(2,1)} async-done(((bf16[96,768]{1,0:T(8,128)(2,1)}), bf16[3072,768]{1,0:T(8,128)(2,1)}) %all-gather.25.cloned.1.call-update) | async-done | bytes 4718608 | tf_op jit(solution)/shard_map/all_gather | solution.py:97
  668.7 8.3 all_to_all.67
  678.9 4.7 convolution_convert_fusion.2
  685.5 68.6 %all-gather.33.cloned.1.call-done = bf16[2,8192,1,192]{3,1,2,0:T(8,128)(2,1)} async-done(((bf16[2,256,1,192]{3,1,2,0:T(8,128)(2,1)}), bf16[2,8192,1,192]{3,1,2,0:T(8,128)(2,1)}) %all-gather.33.cloned.1.call-update) | async-done | bytes 6291472 | tf_op jit(solution)/shard_map/all_gather | solution.py:299
  754.1 10.1 copy.150
  764.3 83.4 %all_gather.71 = f32[2,3,8192]{2,1,0:T(4,128)} all-gather(f32[2,3,256]{2,1,0:T(4,128)S(1)} %log_add_fusion), channel_id=1, replica_groups=mesh['wide'=32,'narrow'=4] {'wide'}, dimensions={2}, use_global_device_ids=true | all-gather | bytes 202752 | tf_op jit(solution)/shard_map/all_gather | solution.py:231
  852.4 96.0 %while.40 = (s32[]{:T(128)}, f32[2,256,3,64]{1,3,2,0:T(8,128)S(1)}, s32[8]{0:T(128)S(1)}, bf16[2,8192,192]{1,2,0:T(8,128)(2,1)}, s32[2]{0:T(128)S(1)}, /*index=5...) while((s32[]{:T(128)}, f32[2,256,3,64]{1,3,2,0:T(8,128)S(1)}, ...), condition=%wide.region_14.15_spmd.clone, body=%wide.region_13.14_spmd.clone.sunk | while | flops 613714944 | bytes 19292376 | solution.py:69
  859.0 5.4 fusion.160
  871.0 5.4 fusion.160
  883.0 5.4 fusion.160
  895.0 5.4 fusion.160
  907.0 5.4 fusion.160
  919.0 5.4 fusion.160
  930.9 5.4 fusion.160
  942.9 5.5 fusion.160
  948.4 29.7 %reduce-scatter.20.cloned.1.call-done = bf16[24,768]{1,0:T(8,128)(2,1)} async-done(((bf16[768,768]{1,0:T(8,128)(2,1)}), bf16[24,768]{1,0:T(8,128)(2,1)}) %reduce-scatter.20.cloned.1.call-update) | async-done | bytes 36880 | tf_op jit(solution)/shard_map/reduce_scatter | solution.py:329
  979.7 79.4 %all_gather.73 = f32[2,3,8192]{2,1,0:T(4,128)S(1)} all-gather(f32[2,3,256]{2,1,0:T(4,128)S(1)} %get-tuple-element.1041), channel_id=1, replica_groups=mesh['wide'=32,'narrow'=4] {'wide'}, dimensions={2}, use_global_device_ids=true | all-gather | bytes 202752 | tf_op jit(solution)/shard_map/all_gather | solution.py:232
  1059.1 150.8 %reduce-scatter.30.cloned.1.call-done = bf16[96,768]{1,0:T(8,128)(2,1)} async-done(((bf16[3072,768]{1,0:T(8,128)(2,1)}), bf16[96,768]{1,0:T(8,128)(2,1)}) %reduce-scatter.30.cloned.1.call-update) | async-done | bytes 147472 | tf_op jit(solution)/shard_map/reduce_scatter | solution.py:338
  1211.7 104.4 %all-gather.27.cloned.1.call-done = bf16[2,8192,192]{2,1,0:T(8,128)(2,1)} async-done(((bf16[2,256,192]{2,1,0:T(8,128)(2,1)}), bf16[2,8192,192]{2,1,0:T(8,128)(2,1)}) %all-gather.27.cloned.1.call-update) | async-done | bytes 6291472 | tf_op jit(solution)/shard_map/all_gather | solution.py:300
  1316.1 10.1 copy.151
  1326.2 139.3 %while.41 = (s32[]{:T(128)}, f32[2,256,3,64]{1,3,2,0:T(8,128)S(1)}, f32[2,256,3,64]{1,3,2,0:T(8,128)}, s32[8]{0:T(128)S(1)}, bf16[2,8192,192]{1,2,0:T(8,128)(2,1...) while((s32[]{:T(128)}, f32[2,256,3,64]{1,3,2,0:T(8,128)S(1)}, ...), condition=%wide.region_16.17_spmd.clone, body=%wide.region_15.16_spmd.clone.sunk | while | flops 821527040 | bytes 27306728 | solution.py:69
  1333.5 4.4 fusion.170
  1337.9 5.5 fusion.169
  1350.8 4.6 fusion.170
  1355.3 5.5 fusion.169
  1368.2 4.6 fusion.170
  1372.8 5.6 fusion.169
  1385.7 4.6 fusion.170
  1390.3 5.5 fusion.169
  1403.1 4.6 fusion.170
  1407.7 5.5 fusion.169
  1420.6 4.6 fusion.170
  1425.2 5.5 fusion.169
  1438.0 4.6 fusion.170
  1442.6 5.5 fusion.169
  1455.4 4.6 fusion.170
  1459.9 5.5 fusion.169
  1468.4 4.5 all-to-all-start.3
  1472.9 74.6 %reduce-scatter.22.cloned.1.call-done = bf16[24,3072]{1,0:T(8,128)(2,1)} async-done(((bf16[768,3072]{1,0:T(8,128)(2,1)}), bf16[24,3072]{1,0:T(8,128)(2,1)}) %reduce-scatter.22.cloned.1.call-update) | async-done | bytes 147472 | tf_op jit(solution)/shard_map/reduce_scatter | solution.py:332
  1547.6 231.9 %reduce-scatter.26.cloned.1.call-done = bf16[24,3072]{1,0:T(8,128)(2,1)} async-done(((bf16[768,3072]{1,0:T(8,128)(2,1)}), bf16[24,3072]{1,0:T(8,128)(2,1)}) %reduce-scatter.26.cloned.1.call-update) | async-done | bytes 147472 | tf_op jit(solution)/shard_map/reduce_scatter | solution.py:335
  1784.7 5.9 copy.159
  1794.7 80.1 %all-reduce = bf16[4,768]{1,0:T(4,128)(2,1)S(1)} all-reduce(bf16[4,768]{1,0:T(4,128)(2,1)S(1)} %pad_maximum_fusion.8), channel_id=15, replica_groups=mesh['wide'=32,'narrow'=4] {'wide'}, use_global_device_ids=true, to_apply=%region_31.32.clone | all-reduce | flops 3072 | bytes 12288
  1874.9 21.3 %all-reduce.1 = bf16[4,24]{1,0:T(4,128)(2,1)S(1)} all-reduce(bf16[4,24]{1,0:T(4,128)(2,1)S(1)} %constant_dynamic-slice_fusion.9), channel_id=16, replica_groups=mesh['wide'=32,'narrow'=4] {'narrow'}, use_global_device_ids=true, to_apply=%region_32.33.clone | all-reduce | flops 96 | bytes 384
  1904.7 185.3 %reduce-scatter.32.cloned.1.call-done = bf16[24,2304]{1,0:T(8,128)(2,1)} async-done(((bf16[768,2304]{1,0:T(8,128)(2,1)}), bf16[24,2304]{1,0:T(8,128)(2,1)}) %reduce-scatter.32.cloned.1.call-update) | async-done | bytes 110608
  2095.1 15.2 reduce-scatter.18.cloned.1.call-done
  (440 shorter events, 278.3 us)
Async XLA Ops:
  7.2 86.2 %all-gather.17.cloned.1.call-start = ((), (), s32[]{:S(2)}) async-start(), calls=%async_computation.14 | async-start | bytes 3649536 | tf_op jit(solution)/shard_map/all_gather | solution.py:93
  14.9 214.5 %all-gather.29.cloned.1.call-start = ((), (), s32[]{:S(2)}) async-start(), calls=%async_computation.27 | async-start | bytes 8650752 | tf_op jit(solution)/shard_map/all_gather | solution.py:171
  100.9 17.3 copy-start.29
  100.9 23.9 %copy-start.23 = (bf16[24,768]{1,0:T(8,128)(2,1)S(1)}, bf16[24,768]{1,0:T(8,128)(2,1)}, u32[]{:S(2)}) copy-start(bf16[24,768]{1,0:T(8,128)(2,1)} %param.19) | copy-start | bytes 110596
  101.0 30.0 %copy-start.24 = (bf16[24,768]{1,0:T(8,128)(2,1)S(1)}, bf16[24,768]{1,0:T(8,128)(2,1)}, u32[]{:S(2)}) copy-start(bf16[24,768]{1,0:T(8,128)(2,1)} %param.20) | copy-start | bytes 110596
  101.0 36.0 %copy-start.22 = (bf16[96,192]{1,0:T(8,128)(2,1)S(1)}, bf16[96,192]{1,0:T(8,128)(2,1)}, u32[]{:S(2)}) copy-start(bf16[96,192]{1,0:T(8,128)(2,1)} %param.21) | copy-start | bytes 110596
  101.9 41.7 %copy-start.38 = (bf16[1,24]{1,0:T(2,128)(2,1)S(1)}, bf16[1,24]{1,0:T(2,128)(2,1)}, u32[]{:S(2)}) copy-start(bf16[1,24]{1,0:T(2,128)(2,1)} %param.22) | copy-start | bytes 148
  101.9 125.8 %copy-start.17 = (s32[2]{0:T(128)S(1)}, s32[2]{0:T(128)}, u32[]{:S(2)}) copy-start(s32[2]{0:T(128)} %param.16) | copy-start | bytes 28
  101.9 126.6 %copy-start.10 = (bf16[2,64,768]{2,1,0:T(8,128)(2,1)S(1)}, bf16[2,64,768]{2,1,0:T(8,128)(2,1)}, u32[]{:S(2)}) copy-start(bf16[2,64,768]{2,1,0:T(8,128)(2,1)} %param.23) | copy-start | bytes 589828
  117.5 112.0 %copy-start.7 = (bf16[2,256,1,192]{3,1,2,0:T(8,128)(2,1)}, bf16[2,256,1,192]{3,1,2,0:T(8,128)(2,1)S(1)}, u32[]{:S(2)}) copy-start(bf16[2,256,1,192]{3,1,2,0:T(8,128)(2,1)S(1)} %get-tuple-element.589) | copy-start | bytes 589828
  117.5 208.2 %all-gather.31.cloned.1.call-start = ((), (), s32[]{:S(2)}) async-start(), calls=%async_computation.28 | async-start | bytes 8650752 | tf_op jit(solution)/shard_map/all_gather | solution.py:172
  118.2 331.6 %all-gather.19.cloned.1.call-start = ((), (), s32[]{:S(2)}) async-start(), calls=%async_computation.15 | async-start | bytes 1216512 | tf_op jit(solution)/shard_map/all_gather | solution.py:94
  124.8 353.4 %all-gather.21.cloned.1.call-start = ((), (), s32[]{:S(2)}) async-start(), calls=%async_computation.16 | async-start | bytes 4866048 | tf_op jit(solution)/shard_map/all_gather | solution.py:95
  130.9 432.1 %all-gather.23.cloned.1.call-start = ((), (), s32[]{:S(2)}) async-start(), calls=%async_computation.17 | async-start | bytes 4866048 | tf_op jit(solution)/shard_map/all_gather | solution.py:96
  136.9 511.6 %all-gather.25.cloned.1.call-start = ((), (), s32[]{:S(2)}) async-start(), calls=%async_computation.18 | async-start | bytes 4866048 | tf_op jit(solution)/shard_map/all_gather | solution.py:97
  143.5 610.6 %all-gather.33.cloned.1.call-start = ((), (), s32[]{:S(2)}) async-start(), calls=%async_computation.29 | async-start | bytes 8650752 | tf_op jit(solution)/shard_map/all_gather | solution.py:299
  227.9 424.3 %copy-start.37 = (f32[128]{0:T(128)}, f32[128]{0:T(128)S(1)}, u32[]{:S(2)}) copy-start(f32[128]{0:T(128)S(1)} %reshape.310) | copy-start | bytes 1540
  228.5 420.0 %copy-start.19 = (f32[768]{0:T(1024)}, f32[768]{0:T(1024)S(1)}, u32[]{:S(2)}) copy-start(f32[768]{0:T(1024)S(1)} %get-tuple-element.503) | copy-start | bytes 9220
  228.5 423.7 %copy-start.21 = (f32[768]{0:T(1024)}, f32[768]{0:T(1024)S(1)}, u32[]{:S(2)}) copy-start(f32[768]{0:T(1024)S(1)} %get-tuple-element.500) | copy-start | bytes 9220
  335.8 114.1 %copy-start.9 = (bf16[2,64,768]{2,1,0:T(8,128)(2,1)S(1)}, bf16[2,64,768]{2,1,0:T(8,128)(2,1)}, u32[]{:S(2)}) copy-start(bf16[2,64,768]{2,1,0:T(8,128)(2,1)} %param.15) | copy-start | bytes 589828
  342.1 4.6 copy-start
  354.9 4.7 copy-start
  367.8 4.6 copy-start
  380.7 4.7 copy-start
  393.6 4.6 copy-start
  406.4 4.6 copy-start
  419.3 4.6 copy-start
  432.2 4.7 copy-start
  438.8 43.7 %copy-start.11 = (f32[2,256,3,64]{1,3,2,0:T(8,128)}, f32[2,256,3,64]{1,3,2,0:T(8,128)S(1)}, u32[]{:S(2)}) copy-start(f32[2,256,3,64]{1,3,2,0:T(8,128)S(1)} %get-tuple-element.167) | copy-start | bytes 1179652
  439.8 9.6 all-to-all-start.1
  444.2 533.9 %reduce-scatter.20.cloned.1.call-start = ((), (), s32[]{:S(2)}) async-start(), calls=%async_computation.21 | async-start | bytes 1216512 | tf_op jit(solution)/shard_map/reduce_scatter | solution.py:329
  451.6 197.0 %copy-start.27 = (f32[128]{0:T(128)}, f32[128]{0:T(128)S(1)}, u32[]{:S(2)}) copy-start(f32[128]{0:T(128)S(1)} %broadcast_multiply_fusion.7) | copy-start | bytes 1540
  451.8 196.8 %copy-start.30 = (f32[128]{0:T(128)}, f32[128]{0:T(128)S(1)}, u32[]{:S(2)}) copy-start(f32[128]{0:T(128)S(1)} %add_rsqrt_fusion.1) | copy-start | bytes 1540
  568.1 84.9 %copy-start.26 = (f32[768]{0:T(1024)S(1)}, f32[768]{0:T(1024)}, u32[]{:S(2)}) copy-start(f32[768]{0:T(1024)} %get-tuple-element.501) | copy-start | bytes 9220
  648.6 6.2 slice-start.4
  648.6 6.2 copy-start.13
  648.6 6.2 copy-start.39
  648.6 6.2 slice-start.5
  653.0 3.7 slice-start
  653.0 5.4 slice-start.2
  654.8 2.0 slice-start.1
  654.8 3.7 slice-start.3
  656.6 4.2 copy-start.5
  656.7 1.8 copy-start.20
  656.7 1.8 copy-start.28
  661.1 5.2 copy-start.2
  662.6 547.3 %reduce-scatter.30.cloned.1.call-start = ((), (), s32[]{:S(2)}) async-start(), calls=%async_computation.26 | async-start | bytes 4866048 | tf_op jit(solution)/shard_map/reduce_scatter | solution.py:338
  666.2 649.9 %all-gather.27.cloned.1.call-start = ((), (), s32[]{:S(2)}) async-start(), calls=%async_computation.19 | async-start | bytes 8650752 | tf_op jit(solution)/shard_map/all_gather | solution.py:300
  678.6 5.6 copy-start.36
  678.6 868.8 %reduce-scatter.22.cloned.1.call-start = ((), (), s32[]{:S(2)}) async-start(), calls=%async_computation.22 | async-start | bytes 4866048 | tf_op jit(solution)/shard_map/reduce_scatter | solution.py:332
  683.6 1095.8 %reduce-scatter.26.cloned.1.call-start = ((), (), s32[]{:S(2)}) async-start(), calls=%async_computation.24 | async-start | bytes 4866048 | tf_op jit(solution)/shard_map/reduce_scatter | solution.py:335
  851.3 1046.1 %reduce-scatter.34.cloned.1.call-start = ((), (), s32[]{:S(2)}) async-start(), calls=%async_computation.31 | async-start | bytes 245760
  979.7 919.2 %reduce-scatter.36.cloned.1.call-start = ((), (), s32[]{:S(2)}) async-start(), calls=%async_computation.32 | async-start | bytes 245760
  1211.7 114.5 %copy-start.14 = (f32[2,256,3,64]{1,3,2,0:T(8,128)S(1)}, f32[2,256,3,64]{1,3,2,0:T(8,128)}, u32[]{:S(2)}) copy-start(f32[2,256,3,64]{1,3,2,0:T(8,128)} %custom-call.4) | copy-start | bytes 1179652
  1211.7 114.5 %copy-start.25 = (s32[256]{0:T(256)S(1)}, s32[256]{0:T(256)}, u32[]{:S(2)}) copy-start(s32[256]{0:T(256)} %iota_add_fusion.2) | copy-start | bytes 3076
  1468.4 311.1 %all-to-all-start.3 = ((bf16[2,256,3,192]{3,0,2,1:T(2,128)(2,1)}), bf16[2,256,3,192]{3,0,2,1:T(2,128)(2,1)S(1)}, u32[]{:S(2)}, u32[]{:S(2)}) async-start(bf16[2,256,3,192]{3,0,2,1:T(2,128)(2,1)} %copy.152), calls=%async_computation.3 | async-start | bytes 1572864 | tf_op jit(solution)/shard_map/all_to_all | solution.py:316
  1472.9 429.0 %reduce-scatter.24.cloned.1.call-start = ((), (), s32[]{:S(2)}) async-start(), calls=%async_computation.23 | async-start | bytes 184320 | tf_op jit(solution)/shard_map/reduce_scatter | solution.py:352
  1547.5 355.7 %reduce-scatter.28.cloned.1.call-start = ((), (), s32[]{:S(2)}) async-start(), calls=%async_computation.25 | async-start | bytes 184320 | tf_op jit(solution)/shard_map/reduce_scatter | solution.py:355
  1779.5 310.5 %reduce-scatter.32.cloned.1.call-start = ((), (), s32[]{:S(2)}) async-start(), calls=%async_computation.30 | async-start | bytes 3649536
  1784.7 6.0 copy-start.32
  1784.7 9.9 copy-start.34
  1784.7 9.9 copy-start.33
  1784.7 307.2 %copy-start.1 = (bf16[768,2304]{1,0:T(8,128)(2,1)S(1)}, bf16[768,2304]{1,0:T(8,128)(2,1)}, u32[]{:S(2)}) copy-start(bf16[768,2304]{1,0:T(8,128)(2,1)} %all-gather.17.cloned.1.call-done) | copy-start | bytes 10616836
  1790.7 319.5 %reduce-scatter.18.cloned.1.call-start = ((), (), s32[]{:S(2)}) async-start(), calls=%async_computation.20 | async-start | bytes 737280 | tf_op jit(solution)/shard_map/reduce_scatter | solution.py:346
  (10 other events, 10.8 us)
Sparse Core Ops, SparseCore 0:
  15.1 78.2 all-gather.16
  117.6 103.0 all-gather.28
  223.8 101.8 all-gather.30
  329.1 64.1 all-gather.18
  396.2 81.9 all-gather.20
  481.1 81.9 all-gather.22
  566.6 81.9 all-gather.24
  651.6 102.4 all-gather.32
  758.9 219.1 reduce-scatter.19
  983.8 226.0 reduce-scatter.29
  1213.5 102.5 all-gather.26
  1321.8 225.6 reduce-scatter.21
  1553.4 226.0 reduce-scatter.25
  1781.8 16.4 reduce-scatter.33
  1800.5 18.2 reduce-scatter.35
  1821.1 17.8 reduce-scatter.23
  1841.2 17.9 reduce-scatter.27
  1864.8 225.0 reduce-scatter.31
  2092.5 17.7 reduce-scatter.17
where the time goes:
time: 2130 us; the launch traced here: 2120 us
  waiting for transfers between devices  1220 us (57%)
  blocking collectives  400 us (19%)
  matrix products  289 us (14%)
  local copies, waits for them, and re-layouts  141 us (7%)
  other arithmetic  31.4 us (1%)
    reduce_scatter x1, waiting for transfers between devices, on_device(): lax.psum_scatter(grad_wup.astype(jnp.bfloat16), 'wide', scatter_dimension...  232 us
    unnamed x22, waiting for transfers between devices  186 us
    reduce_scatter x1, waiting for transfers between devices, on_device(): lax.psum_scatter(grad_wdown.astype(jnp.bfloat16), 'wide', scatter_dimensi...  151 us
    all_gather x1, waiting for transfers between devices, on_device(): lax.all_gather(grad_heads, 'wide', axis=1, tiled=True)  104 us
    unnamed x2, blocking collectives  101 us
    all_gather x1, waiting for transfers between devices, on_device(): lax.all_gather(value_flat, 'wide', axis=1, tiled=True)  86 us
    all_gather x1, blocking collectives, on_device(): lax.all_gather(log_sum, 'wide', axis=2, tiled=True)  83.4 us
    all_gather x1, waiting for transfers between devices, on_device(): lax.all_gather(part_up, 'wide', axis=0, tiled=True)  80.5 us
  transfers between devices with their start and end apart: 21, of which 14 were waited for; matrix products, arithmetic and copies ran while one was open for 21% of the time, Pallas kernels for 0%

commit v1 on v0

v1 whole, which is shorter than its diff:
```python
import functools
import math

import jax
import jax.numpy as jnp
from jax import lax
from jax.experimental import pallas as pl
from jax.experimental.pallas import tpu as pltpu
from jax.sharding import Mesh
from jax.sharding import PartitionSpec as P

HEADS = 12
HEAD = 64
EPSILON = 1e-05
AXES = ("y", "z", "xh", "xl", "c")
WIDE = ("y", "z", "xh")
NARROW = ("xl", "c")
QAX = ("z", "xh")
KAX = ("y",)
NQ = 8
NK = 4
LOG2E = math.log2(math.e)
NEG = -1e30
f32 = jnp.float32
bf16 = jnp.bfloat16


def exchange(x, axes):
    return lax.all_to_all(x, axes, 0, 0, tiled=True)


def gather(x, axes, n):
    return exchange(jnp.broadcast_to(x[None], (n,) + x.shape), axes)


def flip(x, axis):
    return lax.ppermute(x, axis, [(0, 1), (1, 0)])


def layer_norm_parts(residual, gain_vec, bias_vec):
    row_mean = jnp.mean(residual, -1, keepdims=True)
    centred = residual - row_mean
    variance = jnp.mean(centred * centred, -1, keepdims=True)
    inv_std = lax.rsqrt(variance + EPSILON)
    unit_rows = centred * inv_std
    return (unit_rows * gain_vec + bias_vec, unit_rows, inv_std)


def norm_back(incoming, unit_rows, inv_std, gain_vec):
    scaled = incoming * gain_vec
    return inv_std * (
        scaled
        - jnp.mean(scaled, -1, keepdims=True)
        - unit_rows * jnp.mean(scaled * unit_rows, -1, keepdims=True)
    )


def sum_to_own(part):
    seqs, slots, width = part.shape
    cells = part.reshape(seqs, 2, 2, slots // 4, width)
    ci, xi = lax.axis_index("c"), lax.axis_index("xl")
    mine = lax.dynamic_index_in_dim(cells, ci, 2, keepdims=False)
    theirs = lax.dynamic_index_in_dim(cells, 1 - ci, 2, keepdims=False)
    half = mine.astype(f32) + flip(theirs.astype(bf16), "c").astype(f32)
    mine = lax.dynamic_index_in_dim(half, xi, 1, keepdims=False)
    theirs = lax.dynamic_index_in_dim(half, 1 - xi, 1, keepdims=False)
    return mine + flip(theirs.astype(bf16), "xl").astype(f32)


def narrow_gather(x):
    return lax.all_gather(x, NARROW, axis=1, tiled=True)


def split3(x):
    hi = x.astype(bf16)
    rest = x - hi.astype(f32)
    mid = rest.astype(bf16)
    low = (rest - mid.astype(f32)).astype(bf16)
    return hi, mid, low


def key_bias(lens_ref, start_ref, seq, tile):
    slot = start_ref[tile] + lax.broadcasted_iota(jnp.int32, (16, 256), 1)
    row = lax.broadcasted_iota(jnp.int32, (16, 256), 0)
    bias = jnp.where(slot < lens_ref[seq], 0.0, NEG)
    return jnp.where(row == 0, bias, jnp.where(row < 4, 1.0, 0.0)).astype(bf16)


def valid_tiles(lens_ref, start_ref, seq):
    n = jnp.int32(0)
    for tile in range(NK):
        n = n + (start_ref[tile] < lens_ref[seq]).astype(jnp.int32)
    return n


def attend_kernel(lens_ref, start_ref, q_ref, kv_ref, out_ref, kx_ref, vx_ref, o_ref, m_ref):
    row = lax.broadcasted_iota(jnp.int32, (16, 256), 0)
    one_row = jnp.where(row == 0, 1.0, 0.0).astype(bf16)
    for seq in range(2):
        for tile in range(NK):
            extra = key_bias(lens_ref, start_ref, seq, tile)
            for h in range(3):
                kt = jnp.concatenate([kv_ref[tile, seq, pl.ds(64 * h, 64), :], extra], 0)
                kx_ref[tile, seq, h] = jnp.transpose(kt)
                vx_ref[tile, seq, h, pl.ds(0, 64), :] = kv_ref[tile, seq, pl.ds(192 + 64 * h, 64), :]
                vx_ref[tile, seq, h, pl.ds(64, 16), :] = one_row
    for seq in range(2):
        tiles = valid_tiles(lens_ref, start_ref, seq)

        @pl.loop(0, NQ)
        def _(block):
            qx = [
                jnp.concatenate([q_ref[block, seq, pl.ds(64 * h, 64), :], one_row], 0)
                for h in range(3)
            ]

            def step(tile, first):
                for h in range(3):
                    s = jnp.dot(kx_ref[tile, seq, h], qx[h], preferred_element_type=f32)
                    peak = jnp.max(s, 0, keepdims=True)
                    if not first:
                        before = m_ref[h, pl.ds(0, 1), :]
                        peak = jnp.maximum(before, peak)
                    p = jnp.exp2(s - peak).astype(bf16)
                    o = jnp.dot(vx_ref[tile, seq, h], p, preferred_element_type=f32)
                    if not first:
                        o = o + o_ref[h] * jnp.exp2(before - peak)
                    o_ref[h] = o
                    m_ref[h, pl.ds(0, 1), :] = peak

            step(0, True)

            @pl.loop(1, tiles)
            def _(tile):
                step(tile, False)

            rows = []
            for h in range(3):
                total = o_ref[h, pl.ds(64, 1), :]
                out_ref[block, seq, pl.ds(64 * h, 64), :] = (
                    o_ref[h, pl.ds(0, 64), :] / total
                ).astype(bf16)
                lse = m_ref[h, pl.ds(0, 1), :] + jnp.log2(total)
                rows += [part.astype(f32) for part in split3(lse)]
            rows.append(jnp.zeros((7, 256), f32))
            out_ref[block, seq, pl.ds(192, 16), :] = jnp.concatenate(rows, 0).astype(bf16)


def attend_back_kernel(
    lens_ref, start_ref, q_ref, kv_ref, g_ref, dq_ref, dkv_ref, kx_ref, vx_ref, dk_ref, dv_ref, acc_ref
):
    row = lax.broadcasted_iota(jnp.int32, (16, 256), 0)
    ones = jnp.where(row < 3, 1.0, 0.0).astype(bf16)
    for seq in range(2):
        for tile in range(NK):
            extra = key_bias(lens_ref, start_ref, seq, tile)
            for h in range(3):
                kt = jnp.concatenate([kv_ref[tile, seq, pl.ds(64 * h, 64), :], extra], 0)
                kx_ref[tile, seq, h] = jnp.transpose(kt)
                vt = jnp.concatenate([kv_ref[tile, seq, pl.ds(192 + 64 * h, 64), :], ones], 0)
                vx_ref[tile, seq, h] = jnp.transpose(vt)
    dk_ref[...] = jnp.zeros_like(dk_ref)
    dv_ref[...] = jnp.zeros_like(dv_ref)
    nt = (((1,), (1,)), ((), ()))
    for seq in range(2):
        tiles = valid_tiles(lens_ref, start_ref, seq)

        @pl.loop(0, NQ)
        def _(block):
            stats = g_ref[block, seq, pl.ds(192, 32), :].astype(f32)
            one = jnp.ones((1, 256), f32)
            q, g, qx, gx = [], [], [], []
            for h in range(3):
                q.append(q_ref[block, seq, pl.ds(64 * h, 64), :])
                g.append(g_ref[block, seq, pl.ds(64 * h, 64), :])
                extra = jnp.concatenate(
                    [one, stats[3 * h : 3 * h + 3], jnp.zeros((12, 256), f32)], 0
                ).astype(bf16)
                qx.append(jnp.concatenate([q[h], extra], 0))
                extra = jnp.concatenate(
                    [stats[16 + 3 * h : 16 + 3 * h + 3], jnp.zeros((13, 256), f32)], 0
                ).astype(bf16)
                gx.append(jnp.concatenate([g[h], extra], 0))

            acc_ref[...] = jnp.zeros_like(acc_ref)

            @pl.loop(0, tiles)
            def _(tile):
                for h in range(3):
                    s = jnp.dot(kx_ref[tile, seq, h], qx[h], preferred_element_type=f32)
                    p = jnp.exp2(s)
                    d = jnp.dot(vx_ref[tile, seq, h], gx[h], preferred_element_type=f32)
                    ds = (p * d).astype(bf16)
                    acc_ref[h] += jnp.dot(
                        kv_ref[tile, seq, pl.ds(64 * h, 64), :], ds, preferred_element_type=f32
                    )
                    dk_ref[tile, seq, h] += lax.dot_general(
                        q[h], ds, nt, preferred_element_type=f32
                    )
                    dv_ref[tile, seq, h] += lax.dot_general(
                        g[h], p.astype(bf16), nt, preferred_element_type=f32
                    )

            for h in range(3):
                dq_ref[block, seq, pl.ds(64 * h, 64), :] = (acc_ref[h] * HEAD**-0.5).astype(bf16)

    for seq in range(2):
        for tile in range(NK):
            for h in range(3):
                dkv_ref[tile, seq, pl.ds(64 * h, 64), :] = (
                    dk_ref[tile, seq, h] * (1.0 / LOG2E)
                ).astype(bf16)
                dkv_ref[tile, seq, pl.ds(192 + 64 * h, 64), :] = dv_ref[tile, seq, h].astype(bf16)


SMEM = pl.BlockSpec(memory_space=pltpu.SMEM)
VMEM = pl.BlockSpec(memory_space=pltpu.VMEM)
PARAMS = pltpu.CompilerParams(vmem_limit_bytes=48 * 1024 * 1024)


def attend(lengths, starts, q_all, kv_all):
    return pl.pallas_call(
        attend_kernel,
        out_shape=jax.ShapeDtypeStruct((NQ, 2, 208, 256), bf16),
        in_specs=[SMEM, SMEM, VMEM, VMEM],
        out_specs=VMEM,
        scratch_shapes=[
            pltpu.VMEM((NK, 2, 3, 256, 80), bf16),
            pltpu.VMEM((NK, 2, 3, 80, 256), bf16),
            pltpu.VMEM((3, 80, 256), f32),
            pltpu.VMEM((3, 8, 256), f32),
        ],
        compiler_params=PARAMS,
        cost_estimate=pl.CostEstimate(
            flops=12_582_912 * 512, bytes_accessed=5_000_000, transcendentals=12_582_912
        ),
    )(lengths, starts, q_all, kv_all)


def attend_back(lengths, starts, q_all, kv_all, g_all):
    return pl.pallas_call(
        attend_back_kernel,
        out_shape=(
            jax.ShapeDtypeStruct((NQ, 2, 192, 256), bf16),
            jax.ShapeDtypeStruct((NK, 2, 384, 256), bf16),
        ),
        in_specs=[SMEM, SMEM, VMEM, VMEM, VMEM],
        out_specs=(VMEM, VMEM),
        scratch_shapes=[
            pltpu.VMEM((NK, 2, 3, 256, 80), bf16),
            pltpu.VMEM((NK, 2, 3, 256, 80), bf16),
            pltpu.VMEM((NK, 2, 3, 64, 256), f32),
            pltpu.VMEM((NK, 2, 3, 64, 256), f32),
            pltpu.VMEM((3, 64, 256), f32),
        ],
        compiler_params=PARAMS,
        cost_estimate=pl.CostEstimate(
            flops=12_582_912 * 1280, bytes_accessed=8_000_000, transcendentals=12_582_912
        ),
    )(lengths, starts, q_all, kv_all, g_all)


def on_device(hidden_in, lengths, w_qkv, w_out, w_gate, w_up, w_down, norm_params, cotangent):
    y_i, z_i, xh_i = (lax.axis_index(a) for a in WIDE)
    wide_i = (y_i * 4 + z_i) * 2 + xh_i
    n_i = lax.axis_index("xl") * 2 + lax.axis_index("c")
    seqs, own_slots, width = hidden_in.shape
    slots = own_slots * 4

    blocks = w_qkv.reshape(24, 3, 192).transpose(1, 0, 2)
    picks = (jnp.arange(4) - 3 * n_i) % 4
    sent = jnp.take(blocks, jnp.minimum(picks, 2), axis=0)
    got = exchange(sent, NARROW)
    sources = (4 * jnp.arange(3) + n_i) // 3
    qkv_mine = jnp.take(got, sources, axis=0).transpose(1, 0, 2).reshape(24, 576)
    wqkv = gather(qkv_mine, WIDE, 32).reshape(width, 576)

    turn_pairs = [
        ((y * 4 + n), (n * 4 + y)) for y in range(4) for n in range(4)
    ]
    down_turned = lax.ppermute(w_down, ("y",) + NARROW, turn_pairs)
    out_rows = narrow_gather(w_out)
    norm_rows = lax.all_gather(norm_params, NARROW, axis=0, tiled=True)
    norm_row = jnp.pad(norm_rows.reshape(1, 96), ((0, 7), (0, width - 96)))
    packed = jnp.concatenate(
        [w_gate, w_up, out_rows, down_turned.reshape(24, width), norm_row], axis=0
    )
    all_weights = gather(packed, WIDE, 32)
    wgate = all_weights[:, 0:24].reshape(width, width)
    wup = all_weights[:, 24:48].reshape(width, width)
    wout = all_weights[:, 48:72].reshape(width, width)
    wdown = (
        all_weights[:, 72:96].reshape(4, 8, 96, 192).transpose(1, 2, 0, 3).reshape(width, width)
    )
    norm_values = (
        all_weights[:, 96, :96].reshape(32, 4, 24).transpose(1, 0, 2).reshape(4, width).astype(f32)
    )

    tokens = narrow_gather(hidden_in)
    positions = wide_i * slots + jnp.arange(slots)
    freqs = 10000.0 ** (-2.0 * jnp.arange(HEAD // 2, dtype=f32) / HEAD)
    angles = freqs[:, None] * positions.astype(f32)[None, :]
    cosine, sine = jnp.cos(angles), jnp.sin(angles)
    projected = jnp.einsum("df,std->sft", wqkv, tokens, preferred_element_type=f32)

    def rotate(block):
        halves = block.reshape(seqs, 3, 2, HEAD // 2, slots)
        first, second = halves[:, :, 0], halves[:, :, 1]
        return jnp.stack(
            [first * cosine - second * sine, second * cosine + first * sine], 2
        ).reshape(seqs, 192, slots)

    query = (rotate(projected[:, :192]) * (HEAD**-0.5 * LOG2E)).astype(bf16)
    keyval = jnp.concatenate(
        [rotate(projected[:, 192:384]), projected[:, 384:]], axis=1
    ).astype(bf16)
    q_all = gather(query, QAX, NQ)
    kv_all = gather(keyval, KAX, NK)
    starts = (jnp.arange(NK) * 8 + z_i * 2 + xh_i).astype(jnp.int32) * slots
    parts = attend(lengths, starts, q_all, kv_all)
    parts = exchange(parts, QAX).astype(f32)
    part_lse = jnp.sum(parts[:, :, 192:201].reshape(NQ, seqs, 3, 3, slots), 3)
    top = jnp.max(part_lse, 0)
    lse = top + jnp.log2(jnp.sum(jnp.exp2(part_lse - top), 0))
    shares = jnp.exp2(part_lse - lse)
    attended = jnp.sum(
        parts[:, :, :192].reshape(NQ, seqs, 3, HEAD, slots) * shares[:, :, :, None, :], 0
    )
    attn_sent = attended.reshape(seqs, 192, slots).astype(bf16)
    attn_all = narrow_gather(attn_sent)

    projection = jnp.einsum("sft,fd->std", attn_all, wout, preferred_element_type=f32)
    normed, _, _ = layer_norm_parts(
        tokens.astype(f32) + projection, norm_values[0], norm_values[1]
    )
    normed_low = normed.astype(bf16)
    own_slice = lambda a: lax.dynamic_slice_in_dim(a, n_i * own_slots, own_slots, 1)
    own_first, unit_first, inv_first = layer_norm_parts(
        hidden_in.astype(f32) + own_slice(projection), norm_values[0], norm_values[1]
    )
    flat_low = normed_low.reshape(-1, width)
    gate_pre = jnp.dot(flat_low, wgate, preferred_element_type=f32)
    up_pre = jnp.dot(flat_low, wup, preferred_element_type=f32)
    gate_sigmoid = jax.nn.sigmoid(gate_pre)
    gate_silu = gate_pre * gate_sigmoid
    activated = (gate_silu * up_pre).astype(bf16)
    down_part = jnp.dot(activated, wdown, preferred_element_type=f32)
    down_out = sum_to_own(down_part.reshape(seqs, slots, width))
    output_rows, unit_second, inv_second = layer_norm_parts(
        own_first + down_out, norm_values[2], norm_values[3]
    )
    own_positions = wide_i * slots + n_i * own_slots + jnp.arange(own_slots)
    valid = (own_positions[None, :] < lengths[:, None]).astype(f32)[:, :, None]
    layer_out = (output_rows * valid).astype(bf16)
    grad_rows = cotangent.astype(f32) * valid
    grad_gain2 = jnp.sum(grad_rows * unit_second, (0, 1))
    grad_bias2 = jnp.sum(grad_rows, (0, 1))
    grad_second = norm_back(grad_rows, unit_second, inv_second, norm_values[2])
    down_low = narrow_gather(grad_second.astype(bf16)).reshape(-1, width)

    grad_wdown = jnp.einsum("tf,td->fd", activated, down_low, preferred_element_type=f32)
    grad_act = jnp.einsum("td,fd->tf", down_low, wdown, preferred_element_type=f32)
    silu_slope = gate_sigmoid * (1.0 + gate_pre * (1.0 - gate_sigmoid))
    grad_gate_low = (grad_act * up_pre * silu_slope).astype(bf16)
    grad_up_low = (grad_act * gate_silu).astype(bf16)
    grad_wgate = jnp.einsum("td,tf->df", flat_low, grad_gate_low, preferred_element_type=f32)
    grad_wup = jnp.einsum("td,tf->df", flat_low, grad_up_low, preferred_element_type=f32)
    first_part = jnp.einsum(
        "tf,df->td", grad_gate_low, wgate, preferred_element_type=f32
    ) + jnp.einsum("tf,df->td", grad_up_low, wup, preferred_element_type=f32)
    grad_normed = grad_second + sum_to_own(first_part.reshape(seqs, slots, width))
    grad_gain1 = jnp.sum(grad_normed * unit_first, (0, 1))
    grad_bias1 = jnp.sum(grad_normed, (0, 1))
    grad_first = norm_back(grad_normed, unit_first, inv_first, norm_values[0])
    res_low = narrow_gather(grad_first.astype(bf16))
    out_mine = lax.dynamic_slice_in_dim(wout, n_i * 192, 192, 0)
    grad_attn = jnp.einsum("fd,std->sft", out_mine, res_low, preferred_element_type=f32).astype(
        bf16
    )
    delta = jnp.sum(
        grad_attn.astype(f32).reshape(seqs, 3, HEAD, slots) * attended, 2
    )

    def three(x):
        hi = lax.reduce_precision(x, 8, 7)
        mid = lax.reduce_precision(x - hi, 8, 7)
        low = x - hi - mid
        return jnp.pad(
            jnp.stack([hi, mid, low], 2).reshape(seqs, 9, slots), ((0, 0), (0, 7), (0, 0))
        )

    sent_back = jnp.concatenate(
        [grad_attn, three(-lse).astype(bf16), three(-delta).astype(bf16)], axis=1
    )
    g_all = gather(sent_back, QAX, NQ)

    res_cols = lax.dynamic_slice_in_dim(res_low, n_i * 192, 192, 2)
    grad_wout = jnp.einsum("sft,std->fd", attn_all, res_cols, preferred_element_type=f32)
    grad_norm_rows = jnp.stack([grad_gain1, grad_bias1, grad_gain2, grad_bias2])
    norm_blocks = grad_norm_rows.reshape(4, 32, 24).transpose(1, 0, 2).reshape(32, 1, 96)
    norm_blocks = jnp.pad(norm_blocks, ((0, 0), (0, 1), (0, width - 96)))
    grads_packed = jnp.concatenate(
        [
            grad_wgate.reshape(32, 24, width),
            grad_wup.reshape(32, 24, width),
            grad_wdown.reshape(8, 96, 4, 192).transpose(2, 0, 1, 3).reshape(32, 24, width),
            grad_wout.reshape(32, 6, width),
            norm_blocks,
        ],
        axis=1,
    ).astype(bf16)
    grads_got = jnp.sum(exchange(grads_packed, WIDE).astype(f32), 0)
    sum_gate = grads_got[0:24]
    sum_up = grads_got[24:48]
    sum_down = lax.ppermute(
        grads_got[48:72].reshape(96, 192).astype(bf16), ("y",) + NARROW, turn_pairs
    ).astype(f32)
    sum_out = grads_got[72:78].reshape(24, 192)
    norm_sums = grads_got[78, :96].reshape(4, 24)

    dq_parts, dkv_parts = attend_back(lengths, starts, q_all, kv_all, g_all)
    grad_query = jnp.sum(exchange(dq_parts, QAX).astype(f32), 0)
    grad_keyval = jnp.sum(exchange(dkv_parts, KAX).astype(f32), 0)

    def unrotate(block):
        halves = block.reshape(seqs, 3, 2, HEAD // 2, slots)
        first, second = halves[:, :, 0], halves[:, :, 1]
        return jnp.stack(
            [first * cosine + second * sine, second * cosine - first * sine], 2
        ).reshape(seqs, 192, slots)

    grad_proj = jnp.concatenate(
        [unrotate(grad_query), unrotate(grad_keyval[:, :192]), grad_keyval[:, 192:]], axis=1
    ).astype(bf16)
    grad_wqkv = jnp.einsum("std,sft->df", tokens, grad_proj, preferred_element_type=f32)
    input_part = jnp.einsum("sft,df->std", grad_proj, wqkv, preferred_element_type=f32)
    grad_input = (grad_first + sum_to_own(input_part)).astype(bf16)
    qkv_got = jnp.sum(
        exchange(grad_wqkv.reshape(32, 24, 576).astype(bf16), WIDE).astype(f32), 0
    )
    back = qkv_got.reshape(24, 3, 192).transpose(1, 0, 2)
    where = (sources[None, :] == jnp.arange(4)[:, None]).astype(f32)
    back_sent = jnp.einsum("sk,kdf->sdf", where, back)
    norm_sent = jnp.pad(norm_sums[:, None, :], ((0, 0), (0, 7), (0, 168)))
    back_got = exchange(jnp.concatenate([back_sent, norm_sent], 1).astype(bf16), NARROW).astype(f32)
    sum_norms = jnp.sum(back_got[:, 24, :24], 0)[None]
    order = (3 * n_i + jnp.arange(3)) % 4
    sum_qkv = jnp.take(back_got[:, :24], order, axis=0).transpose(1, 0, 2).reshape(24, 576)
    return (layer_out, grad_input, sum_qkv, sum_out, sum_gate, sum_up, sum_down, sum_norms)


def solution(mesh):
    fine = Mesh(mesh.devices.reshape(4, 4, 2, 2, 2), AXES)
    token = P(None, WIDE + NARROW, None)
    weight = P(WIDE, NARROW)
    norm = P(NARROW, WIDE)
    return jax.shard_map(
        on_device,
        mesh=fine,
        in_specs=(token, P(), weight, weight, weight, weight, weight, norm, token),
        out_specs=(token, token, weight, weight, weight, weight, weight, norm),
        check_vma=False,
    )
```

time: 2130 us -> 637 us (0.30)
  waiting for transfers between devices: 1220 us -> 97 us
  matrix products: 289 us -> 24 us
  blocking collectives: 400 us -> 177 us
  Pallas kernels: 0 us -> 129 us
  starting transfers between devices: 10 us -> 97.1 us
  local copies, waits for them, and re-layouts: 141 us -> 90.3 us
    all_gather x9 -> x0, waiting for transfers between devices: 523 us -> none  [the longest x1 104 us: on_device(): lax.all_gather(grad_heads, 'wide', axis=1, tiled=True)]
    reduce_scatter x7 -> x0, waiting for transfers between devices: 502 us -> none  [the longest x1 232 us: on_device(): lax.psum_scatter(grad_wup.astype(jnp.bfloat16), 'wide', scatter_dimension...]
    dot_general x69 -> x14, matrix products: 285 us -> 22.4 us  [the longest x1 3.29 us: on_device(): jnp.einsum('td,tf->df', flat_low, grad_up_low, preferred_element_type=f32)]
    unnamed x22 -> x0, waiting for transfers between devices: 186 us -> none
    all_gather x9 -> x6, blocking collectives: 277 us -> 123 us  [the longest x5 118 us: narrow_gather(): return lax.all_gather(x, NARROW, axis=1, tiled=True)]
    pallas_call x0 -> x2, Pallas kernels: none -> 129 us  [the longest x1 69.8 us: attend_back(): pl.pallas_call(attend_back_kernel, out_shape=(jax.ShapeDtypeStruct((NQ, 2...]
    unnamed x2 -> x0, blocking collectives: 101 us -> none
    all_to_all x2 -> x10, waiting for transfers between devices: 4.9 us -> 86.9 us  [exchange(): return lax.all_to_all(x, axes, 0, 0, tiled=True)]
  transfers between devices with their start and end apart: 21 -> 18, of which waited for: 14 -> 11; matrix products, arithmetic and copies ran while one was open for 21% -> 13% of each run, Pallas kernels for 0% -> 0%
where the time goes in v1:
time: 637 us; the launch traced here: 643 us
  blocking collectives  177 us (28%)
  Pallas kernels  129 us (20%)
  starting transfers between devices  97.1 us (15%)
  waiting for transfers between devices  97 us (15%)
  local copies, waits for them, and re-layouts  90.3 us (14%)
  other arithmetic  26.5 us (4%)
  matrix products  24 us (4%)
    all_gather x5, blocking collectives, narrow_gather(): return lax.all_gather(x, NARROW, axis=1, tiled=True)  118 us
    all_to_all x10, waiting for transfers between devices, exchange(): return lax.all_to_all(x, axes, 0, 0, tiled=True)  86.9 us
    all_to_all x10, starting transfers between devices, exchange(): return lax.all_to_all(x, axes, 0, 0, tiled=True)  71.1 us
    pallas_call x1, Pallas kernels, attend_back(): pl.pallas_call(attend_back_kernel, out_shape=(jax.ShapeDtypeStruct((NQ, 2...  69.8 us
    pallas_call x1, Pallas kernels, attend(): pl.pallas_call(attend_kernel, out_shape=jax.ShapeDtypeStruct((NQ, 2, 208,...  59.4 us
    all_to_all x2, blocking collectives, exchange(): return lax.all_to_all(x, axes, 0, 0, tiled=True)  53.9 us
    concatenate x1, local copies, waits for them, and re-layouts, on_device(): jnp.concatenate([grad_wgate.reshape(32, 24, width), grad_wup.reshape(32,...  20.2 us
  transfers between devices with their start and end apart: 18, of which 11 were waited for; matrix products, arithmetic and copies ran while one was open for 13% of the time, Pallas kernels for 0%

profile of v1, /device:TPU:1, one launch (start us, length us, event | category | flops | bytes accessed | tf_op | source)
XLA Modules:
  0.0 643.2 jit_solution(14012846552078217314)
XLA Ops:
  2.8 4.7 all-to-all-start
  7.5 3.2 all-to-all-done
  12.5 10.6 %all-to-all-start.1 = ((bf16[32,24,576]{2,1,0:T(8,128)(2,1)}), bf16[32,24,576]{2,1,0:T(8,128)(2,1)S(1)}, u32[]{:S(2)}, u32[]{:S(2)}) async-start(bf16[32,24,576]{2,1,0:T(8,128)(2,1)} %broadcast_in_dim.46), calls=%async_computation.1 | async-start | bytes 1966080 | tf_op jit(solution)/shard_map/all_to_all | solution.py:29
  23.4 16.0 %all_gather.18 = bf16[2,256,768]{2,1,0:T(8,128)(2,1)S(1)} all-gather(bf16[2,64,768]{2,1,0:T(8,128)(2,1)S(1)} %copy-done.36), channel_id=1, replica_groups=mesh['y'=4,'z'=4,'xh'=2,'xl'=2,'c'=2] {'xl','c'}, dimensions={1}, use_global_device_ids=true | all-gather | bytes 983040 | tf_op jit(solution)/shard_map/all_gather | solution.py:71
  42.9 3.6 all-to-all-start.3
  46.5 16.4 %all-to-all-done.3.kv_ref = bf16[4,2,384,256]{3,2,1,0:T(8,128)(2,1)S(1)} async-done(((bf16[4,2,384,256]{3,2,1,0:T(8,128)(2,1)}), bf16[4,2,384,256]{3,2,1,0:T(8,128)(2,1)S(1)}, u32[]{:S(2)}, u32[]{:S(2)}) %all-to-all-start.3) | async-done | bytes 1572896 | tf_op jit(solution)/shard_map/all_to_all | solution.py:29
  62.9 1.4 broadcast_in_dim.47
  64.4 11.0 %all-to-all-start.2 = ((bf16[8,2,192,256]{3,2,1,0:T(8,128)(2,1)}), bf16[8,2,192,256]{3,2,1,0:T(8,128)(2,1)S(1)}, u32[]{:S(2)}, u32[]{:S(2)}) async-start(bf16[8,2,192,256]{3,2,1,0:T(8,128)(2,1)} %broadcast_in_dim.47), calls=%async_computation.2 | async-start | bytes 3145728 | tf_op jit(solution)/shard_map/all_to_all | solution.py:29
  75.3 21.3 %all-to-all-done.2.q_ref = bf16[8,2,192,256]{3,2,1,0:T(8,128)(2,1)S(1)} async-done(((bf16[8,2,192,256]{3,2,1,0:T(8,128)(2,1)}), bf16[8,2,192,256]{3,2,1,0:T(8,128)(2,1)S(1)}, u32[]{:S(2)}, u32[]{:S(2)}) %all-to-all-start.2) | async-done | bytes 1572896 | tf_op jit(solution)/shard_map/all_to_all | solution.py:29
  96.6 59.4 %shard_map.152 = bf16[8,2,208,256]{3,2,1,0:T(8,128)(2,1)} custom-call(s32[2]{0:T(128)S(1)} %copy-done.1, s32[4]{0:T(128)S(1)} %add_multiply_fusion.start_ref, bf16[8,2,192,256]{3,2,1,0:T(8,128)(2,1)S(1)} %all-to-all-done.2.q_ref, bf16[4,2,384,256]{3,2,1,0:T(8,128)(2,1)S(1)} %all-to-all-done.3.kv_ref), custom_call_target="tpu_custom_call" | custom-call | flops 6442450944 | bytes 5000000 | tf_op jit(solution)/shard_map/pallas_call | solution.py:222
  156.0 3.7 all-to-all-start.4
  159.7 4.6 collective-permute-start
  164.4 18.4 %all-gather = bf16[4,192,24]{1,2,0:T(8,128)(2,1)S(1)} all-gather(bf16[1,192,24]{1,2,0:T(8,128)(2,1)S(1)} %bitcast.235), channel_id=1, replica_groups=mesh['y'=4,'z'=4,'xh'=2,'xl'=2,'c'=2] {'xl','c'}, dimensions={0}, use_global_device_ids=true | all-gather | bytes 46080 | tf_op jit(solution)/shard_map/all_gather | solution.py:71
  184.5 5.0 all-gather.1
  189.8 2.6 broadcast_in_dim.49
  192.4 7.7 %all-to-all-start.5 = ((bf16[32,104,768]{2,1,0:T(8,128)(2,1)}), bf16[32,104,768]{2,1,0:T(8,128)(2,1)}, u32[]{:S(2)}, u32[]{:S(2)}) async-start(bf16[32,104,768]{2,1,0:T(8,128)(2,1)} %broadcast_in_dim.49), calls=%async_computation.5 | async-start | bytes 10223616 | tf_op jit(solution)/shard_map/all_to_all | solution.py:29
  203.1 65.0 %all_gather.19 = bf16[2,768,256]{2,1,0:T(8,128)(2,1)} all-gather(bf16[2,192,256]{2,1,0:T(8,128)(2,1)S(1)} %convert_element_type.195), channel_id=1, replica_groups=mesh['y'=4,'z'=4,'xh'=2,'xl'=2,'c'=2] {'xl','c'}, dimensions={1}, use_global_device_ids=true | all-gather | bytes 983040 | tf_op jit(solution)/shard_map/all_gather | solution.py:71
  268.1 8.0 %all-to-all-done.5 = bf16[32,104,768]{2,1,0:T(8,128)(2,1)} async-done(((bf16[32,104,768]{2,1,0:T(8,128)(2,1)}), bf16[32,104,768]{2,1,0:T(8,128)(2,1)}, u32[]{:S(2)}, u32[]{:S(2)}) %all-to-all-start.5) | async-done | bytes 5111840 | tf_op jit(solution)/shard_map/all_to_all | solution.py:29
  278.0 4.2 fusion.66
  282.2 2.4 reshape.617
  284.7 2.6 copy.134
  287.3 2.2 reshape.664
  289.5 2.7 fusion.14
  295.2 2.0 multiply_convert_fusion.2
  299.2 2.3 collective-permute-start.1
  302.2 2.2 reshape.618
  307.5 5.7 collective-permute-start.2
  313.3 5.3 collective-permute-done.2
  320.1 9.5 %all_gather.22 = bf16[2,256,768]{2,1,0:T(8,128)(2,1)S(1)} all-gather(bf16[2,64,768]{2,1,0:T(8,128)(2,1)S(1)} %fusion.39), channel_id=1, replica_groups=mesh['y'=4,'z'=4,'xh'=2,'xl'=2,'c'=2] {'xl','c'}, dimensions={1}, use_global_device_ids=true | all-gather | bytes 983040 | tf_op jit(solution)/shard_map/all_gather | solution.py:71
  334.9 1.7 collective-permute-done.3
  340.8 1.4 add.401
  342.2 3.1 collective-permute-done.4
  345.2 2.4 multiply_reduce_fusion.2
  349.1 8.9 %all_gather.23 = bf16[2,256,768]{2,1,0:T(8,128)(2,1)S(1)} all-gather(bf16[2,64,768]{2,1,0:T(8,128)(2,1)S(1)} %fusion.42), channel_id=1, replica_groups=mesh['y'=4,'z'=4,'xh'=2,'xl'=2,'c'=2] {'xl','c'}, dimensions={1}, use_global_device_ids=true | all-gather | bytes 983040 | tf_op jit(solution)/shard_map/all_gather | solution.py:71
  359.0 1.4 convert_multiply_fusion
  360.7 31.1 %all_to_all.60.g_ref = bf16[8,2,224,256]{3,2,1,0:T(8,128)(2,1)} all-to-all(bf16[8,2,224,256]{3,2,1,0:T(8,128)(2,1)S(1)} %broadcast_in_dim.50), channel_id=1, replica_groups=mesh['y'=4,'z'=4,'xh'=2,'xl'=2,'c'=2] {'z','xh'}, dimensions={0} | all-to-all | bytes 3670016 | tf_op jit(solution)/shard_map/all_to_all | solution.py:29
  391.8 69.8 %shard_map.153 = (bf16[8,2,192,256]{3,2,1,0:T(8,128)(2,1)}, bf16[4,2,384,256]{3,2,1,0:T(8,128)(2,1)S(1)}) custom-call(s32[2]{0:T(128)S(1)} %copy-done.1, s32[4]{0:T(128)S(1)} %add_multiply_fusion.start_ref, bf16[8,2,192,256]{3,2,1,0:T(8,128)(2,1)S(1)} %all-to-all-done.2.q_ref, bf16[4,2,384,256]{3,2,1,0:T(8,128)(2,1)} %copy-done, ...), custom_call_target="tpu_custom_call" | custom-call | flops 16106127360 | bytes 8000000 | tf_op jit(solution)/shard_map/pallas_call | solution.py:241
  461.5 22.9 %all_to_all.61 = bf16[4,2,384,256]{3,2,1,0:T(8,128)(2,1)S(1)} all-to-all(bf16[4,2,384,256]{3,2,1,0:T(8,128)(2,1)S(1)} %get-tuple-element.11), channel_id=1, replica_groups=mesh['y'=4,'z'=4,'xh'=2,'xl'=2,'c'=2] {'y'}, dimensions={0} | all-to-all | bytes 3145728 | tf_op jit(solution)/shard_map/all_to_all | solution.py:29
  484.4 3.8 all-to-all-start.7
  488.2 3.2 fusion.1
  491.5 2.3 copy.150
  493.8 2.3 copy.151
  496.8 1.4 stack.61
  498.2 2.3 copy.152
  500.5 2.4 fusion.6
  504.2 3.9 reshape.627
  508.1 3.3 convolution_convert_fusion.1
  511.4 1.8 convolution_convert_fusion.2
  513.2 1.4 stack.58
  514.6 1.4 stack.59
  517.3 1.5 reshape.675
  518.8 2.5 fusion.8
  521.3 1.9 copy.155
  523.2 2.2 reshape.628
  525.4 1.4 pad.26
  526.8 20.2 %concatenate.35 = bf16[32,80,768]{2,1,0:T(8,128)(2,1)} concatenate(bf16[32,24,768]{2,1,0:T(8,128)(2,1)} %convolution_convert_fusion.2, bf16[32,24,768]{2,1,0:T(8,128)(2,1)} %convolution_convert_fusion.1, bf16[32,24,768]{2,1,0:T(8,128)(2,1)} %reshape.627, bf16[32,6,768]{2,1,0:T(8,128)(2,1)} %reshape.628, bf16[32,2,768]{2,1,0:T(2,128)(2,1)} %pad.26), dimensions={1} | concatenate | bytes 7864320 | tf_op jit(solution)/shard_map/concatenate | solution.py:402
  547.1 7.7 %all-to-all-start.10 = ((bf16[32,80,768]{2,1,0:T(8,128)(2,1)}), bf16[32,80,768]{2,1,0:T(8,128)(2,1)}, u32[]{:S(2)}, u32[]{:S(2)}) async-start(bf16[32,80,768]{2,1,0:T(8,128)(2,1)} %concatenate.35), calls=%async_computation.10 | async-start | bytes 7864320 | tf_op jit(solution)/shard_map/all_to_all | solution.py:29
  558.0 2.0 fusion.71
  560.8 3.1 collective-permute-start.5
  569.1 35.1 %all-to-all-done.10 = bf16[32,80,768]{2,1,0:T(8,128)(2,1)} async-done(((bf16[32,80,768]{2,1,0:T(8,128)(2,1)}), bf16[32,80,768]{2,1,0:T(8,128)(2,1)}, u32[]{:S(2)}, u32[]{:S(2)}) %all-to-all-start.10) | async-done | bytes 3932192 | tf_op jit(solution)/shard_map/all_to_all | solution.py:29
  604.2 5.2 all-to-all-start.9
  610.4 2.7 convert_reduce_fusion
  613.4 9.3 %collective-permute-start.7 = (bf16[96,192]{1,0:T(8,128)(2,1)S(1)}, bf16[96,192]{1,0:T(8,128)(2,1)S(1)}, u32[]{:S(2)}, u32[]{:S(2)}) collective-permute-start(bf16[96,192]{1,0:T(8,128)(2,1)S(1)} %convert_element_type.240), channel_id=1, source_target_pairs={{0,0},{1,32},{2,64},{3,96},{32,1},{33,33},{34,65},{35,97},{64,2},{... | collective-permute-start | bytes 110600 | tf_op jit(solution)/shard_map/ppermute | solution.py:415
  624.5 13.1 %all-to-all-start.11 = ((bf16[4,32,192]{2,1,0:T(8,128)(2,1)}), bf16[4,32,192]{2,1,0:T(8,128)(2,1)S(1)}, u32[]{:S(2)}, u32[]{:S(2)}) async-start(bf16[4,32,192]{2,1,0:T(8,128)(2,1)} %copy.158), calls=%async_computation.11 | async-start | bytes 131072 | tf_op jit(solution)/shard_map/all_to_all | solution.py:29
  (278 shorter events, 57.1 us)
Async XLA Ops:
  2.8 7.9 %all-to-all-start = ((bf16[4,24,192]{2,1,0:T(8,128)(2,1)}), bf16[4,24,192]{2,1,0:T(8,128)(2,1)S(1)}, u32[]{:S(2)}, u32[]{:S(2)}) async-start(bf16[4,24,192]{2,1,0:T(8,128)(2,1)} %broadcast_select_fusion), calls=%async_computation | async-start | bytes 98304 | tf_op jit(solution)/shard_map/all_to_all | solution.py:29
  11.4 12.0 %copy-start.36 = (bf16[2,64,768]{2,1,0:T(8,128)(2,1)S(1)}, bf16[2,64,768]{2,1,0:T(8,128)(2,1)}, u32[]{:S(2)}) copy-start(bf16[2,64,768]{2,1,0:T(8,128)(2,1)} %param.9) | copy-start | bytes 589828
  12.5 27.9 %all-to-all-start.1 = ((bf16[32,24,576]{2,1,0:T(8,128)(2,1)}), bf16[32,24,576]{2,1,0:T(8,128)(2,1)S(1)}, u32[]{:S(2)}, u32[]{:S(2)}) async-start(bf16[32,24,576]{2,1,0:T(8,128)(2,1)} %broadcast_in_dim.46), calls=%async_computation.1 | async-start | bytes 1966080 | tf_op jit(solution)/shard_map/all_to_all | solution.py:29
  23.4 18.0 %copy-start.38 = (f32[32,256]{1,0:T(8,128)}, f32[32,256]{1,0:T(8,128)S(1)}, u32[]{:S(2)}) copy-start(f32[32,256]{1,0:T(8,128)S(1)} %get-tuple-element.60) | copy-start | bytes 98308
  23.4 18.0 %copy-start.40 = (f32[32,256]{1,0:T(8,128)}, f32[32,256]{1,0:T(8,128)S(1)}, u32[]{:S(2)}) copy-start(f32[32,256]{1,0:T(8,128)S(1)} %get-tuple-element.61) | copy-start | bytes 98308
  39.4 1.8 copy-start.2
  42.9 20.0 %all-to-all-start.3 = ((bf16[4,2,384,256]{3,2,1,0:T(8,128)(2,1)}), bf16[4,2,384,256]{3,2,1,0:T(8,128)(2,1)S(1)}, u32[]{:S(2)}, u32[]{:S(2)}) async-start(bf16[4,2,384,256]{3,2,1,0:T(8,128)(2,1)} %broadcast_in_dim.48), calls=%async_computation.3 | async-start | bytes 3145728 | tf_op jit(solution)/shard_map/all_to_all | solution.py:29
  62.9 33.7 %copy-start = (bf16[4,2,384,256]{3,2,1,0:T(8,128)(2,1)}, bf16[4,2,384,256]{3,2,1,0:T(8,128)(2,1)S(1)}, u32[]{:S(2)}) copy-start(bf16[4,2,384,256]{3,2,1,0:T(8,128)(2,1)S(1)} %all-to-all-done.3.kv_ref) | copy-start | bytes 4718596
  64.4 32.3 %copy-start.1 = (s32[2]{0:T(128)S(1)}, s32[2]{0:T(128)}, u32[]{:S(2)}) copy-start(s32[2]{0:T(128)} %lens_ref.3) | copy-start | bytes 28
  64.4 32.3 %all-to-all-start.2 = ((bf16[8,2,192,256]{3,2,1,0:T(8,128)(2,1)}), bf16[8,2,192,256]{3,2,1,0:T(8,128)(2,1)S(1)}, u32[]{:S(2)}, u32[]{:S(2)}) async-start(bf16[8,2,192,256]{3,2,1,0:T(8,128)(2,1)} %broadcast_in_dim.47), calls=%async_computation.2 | async-start | bytes 3145728 | tf_op jit(solution)/shard_map/all_to_all | solution.py:29
  156.0 8.3 %copy-start.52 = (bf16[24,192]{1,0:T(8,128)(2,1)S(1)}, bf16[24,192]{1,0:T(8,128)(2,1)}, u32[]{:S(2)}) copy-start(bf16[24,192]{1,0:T(8,128)(2,1)} %param.12) | copy-start | bytes 27652
  156.0 28.5 %copy-start.58 = (bf16[1,24]{1,0:T(2,128)(2,1)S(1)}, bf16[1,24]{1,0:T(2,128)(2,1)}, u32[]{:S(2)}) copy-start(bf16[1,24]{1,0:T(2,128)(2,1)} %param.16) | copy-start | bytes 148
  156.0 33.8 %all-to-all-start.4 = ((bf16[8,2,208,256]{3,2,1,0:T(8,128)(2,1)}), bf16[8,2,208,256]{3,2,1,0:T(8,128)(2,1)S(1)}, u32[]{:S(2)}, u32[]{:S(2)}) async-start(bf16[8,2,208,256]{3,2,1,0:T(8,128)(2,1)} %shard_map.152), calls=%async_computation.4 | async-start | bytes 3407872 | tf_op jit(solution)/shard_map/all_to_all | solution.py:29
  159.7 29.9 %collective-permute-start = (bf16[96,192]{1,0:T(8,128)(2,1)}, bf16[96,192]{1,0:T(8,128)(2,1)S(1)}, u32[]{:S(2)}, u32[]{:S(2)}) collective-permute-start(bf16[96,192]{1,0:T(8,128)(2,1)} %param.15), channel_id=1, source_target_pairs={{0,0},{1,32},{2,64},{3,96},{32,1},{33,33},{34,65},{35,97},{64,2},{... | collective-permute-start | bytes 110600 | tf_op jit(solution)/shard_map/ppermute | solution.py:281
  192.4 83.7 %all-to-all-start.5 = ((bf16[32,104,768]{2,1,0:T(8,128)(2,1)}), bf16[32,104,768]{2,1,0:T(8,128)(2,1)}, u32[]{:S(2)}, u32[]{:S(2)}) async-start(bf16[32,104,768]{2,1,0:T(8,128)(2,1)} %broadcast_in_dim.49), calls=%async_computation.5 | async-start | bytes 10223616 | tf_op jit(solution)/shard_map/all_to_all | solution.py:29
  278.0 14.7 %copy-start.43 = (f32[768]{0:T(1024)}, f32[768]{0:T(1024)S(1)}, u32[]{:S(2)}) copy-start(f32[768]{0:T(1024)S(1)} %add.384) | copy-start | bytes 9220
  289.5 2.7 copy-start.3
  293.0 1.7 copy-start.15
  294.7 2.5 copy-start.20
  295.2 2.0 copy-start.26
  297.2 4.3 copy-start.37
  298.0 1.3 copy-start.27
  299.2 6.9 %collective-permute-start.1 = (bf16[2,2,64,768]{3,2,0,1:T(8,128)(2,1)}, bf16[2,2,64,768]{3,2,0,1:T(8,128)(2,1)}, u32[]{:S(2)}, u32[]{:S(2)}) collective-permute-start(bf16[2,2,64,768]{3,2,0,1:T(8,128)(2,1)} %fusion.18), channel_id=1, source_target_pairs={{0,1},{1,0},{2,3},{3,2},{4,5},{5,4},{6,7},{7,6},{8,9},{9,8},{10,11... | collective-permute-start | bytes 1179656 | tf_op jit(solution)/shard_map/ppermute | solution.py:37
  304.4 14.1 %copy-start.44 = (f32[768]{0:T(1024)S(1)}, f32[768]{0:T(1024)}, u32[]{:S(2)}) copy-start(f32[768]{0:T(1024)} %copy-done.43) | copy-start | bytes 9220
  305.9 12.9 %copy-start.45 = (f32[2,64]{1,0:T(2,128)}, f32[2,64]{1,0:T(2,128)S(1)}, u32[]{:S(2)}) copy-start(f32[2,64]{1,0:T(2,128)S(1)} %broadcast_multiply_fusion.6) | copy-start | bytes 1540
  307.5 11.5 %copy-start.19 = (bf16[2,64,768]{2,1,0:T(8,128)(2,1)S(1)}, bf16[2,64,768]{2,1,0:T(8,128)(2,1)}, u32[]{:S(2)}) copy-start(bf16[2,64,768]{2,1,0:T(8,128)(2,1)} %param.17) | copy-start | bytes 589828
  307.5 11.5 %copy-start.50 = (f32[2,64]{1,0:T(2,128)S(1)}, f32[2,64]{1,0:T(2,128)}, u32[]{:S(2)}) copy-start(f32[2,64]{1,0:T(2,128)} %compare_convert_fusion) | copy-start | bytes 1540
  307.5 22.1 %copy-start.25 = (bf16[768,768]{1,0:T(8,128)(2,1)S(1)}, bf16[768,768]{1,0:T(8,128)(2,1)}, u32[]{:S(2)}) copy-start(bf16[768,768]{1,0:T(8,128)(2,1)} %reshape.618) | copy-start | bytes 3538948
  307.5 11.0 %collective-permute-start.2 = (bf16[2,64,768]{2,1,0:T(8,128)(2,1)S(1)}, bf16[2,64,768]{2,1,0:T(8,128)(2,1)S(1)}, u32[]{:S(2)}, u32[]{:S(2)}) collective-permute-start(bf16[2,64,768]{2,1,0:T(8,128)(2,1)S(1)} %fusion.35), channel_id=1, source_target_pairs={{0,2},{2,0},{1,3},{3,1},{4,6},{6,4},{5,7},{7,5},{8,10},{10,8},{9,1... | collective-permute-start | bytes 589832 | tf_op jit(solution)/shard_map/ppermute | solution.py:37
  313.3 6.8 %copy-start.48 = (f32[2,64]{1,0:T(2,128)}, f32[2,64]{1,0:T(2,128)S(1)}, u32[]{:S(2)}) copy-start(f32[2,64]{1,0:T(2,128)S(1)} %add_rsqrt_fusion.2) | copy-start | bytes 1540
  318.5 11.0 %copy-start.22 = (f32[512,768]{1,0:T(8,128)S(1)}, f32[512,768]{1,0:T(8,128)}, u32[]{:S(2)}) copy-start(f32[512,768]{1,0:T(8,128)} %get-tuple-element.65) | copy-start | bytes 4718596
  318.8 10.8 %copy-start.21 = (f32[512,768]{1,0:T(8,128)S(1)}, f32[512,768]{1,0:T(8,128)}, u32[]{:S(2)}) copy-start(f32[512,768]{1,0:T(8,128)} %copy-done.20) | copy-start | bytes 4718596
  318.8 12.0 %copy-start.47 = (f32[2,64]{1,0:T(2,128)}, f32[2,64]{1,0:T(2,128)S(1)}, u32[]{:S(2)}) copy-start(f32[2,64]{1,0:T(2,128)S(1)} %broadcast_multiply_fusion.5) | copy-start | bytes 1540
  319.0 11.8 %copy-start.51 = (f32[2,64]{1,0:T(2,128)}, f32[2,64]{1,0:T(2,128)S(1)}, u32[]{:S(2)}) copy-start(f32[2,64]{1,0:T(2,128)S(1)} %add_rsqrt_fusion.1) | copy-start | bytes 1540
  319.9 10.9 %copy-start.53 = (f32[2,64]{1,0:T(2,128)}, f32[2,64]{1,0:T(2,128)S(1)}, u32[]{:S(2)}) copy-start(f32[2,64]{1,0:T(2,128)S(1)} %get-tuple-element.68) | copy-start | bytes 1540
  319.9 11.0 %copy-start.54 = (f32[2,64]{1,0:T(2,128)}, f32[2,64]{1,0:T(2,128)S(1)}, u32[]{:S(2)}) copy-start(f32[2,64]{1,0:T(2,128)S(1)} %get-tuple-element.69) | copy-start | bytes 1540
  329.6 1.6 copy-start.24
  331.1 1.5 copy-start.9
  334.7 1.9 collective-permute-start.3
  338.7 6.6 %collective-permute-start.4 = (bf16[2,64,768]{2,1,0:T(8,128)(2,1)}, bf16[2,64,768]{2,1,0:T(8,128)(2,1)S(1)}, u32[]{:S(2)}, u32[]{:S(2)}) collective-permute-start(bf16[2,64,768]{2,1,0:T(8,128)(2,1)} %fusion.36), channel_id=1, source_target_pairs={{0,2},{2,0},{1,3},{3,1},{4,6},{6,4},{5,7},{7,5},{8,10},{10,8},{9,1... | collective-permute-start | bytes 589832 | tf_op jit(solution)/shard_map/ppermute | solution.py:37
  342.2 16.8 %copy-start.12 = (f32[2,192,256]{2,1,0:T(8,128)S(1)}, f32[2,192,256]{2,1,0:T(8,128)}, u32[]{:S(2)}) copy-start(f32[2,192,256]{2,1,0:T(8,128)} %copy-done.11) | copy-start | bytes 1179652
  347.7 12.7 %copy-start.13 = (f32[2,64,768]{2,1,0:T(8,128)}, f32[2,64,768]{2,1,0:T(8,128)S(1)}, u32[]{:S(2)}) copy-start(f32[2,64,768]{2,1,0:T(8,128)S(1)} %get-tuple-element.26) | copy-start | bytes 1179652
  349.1 11.4 %copy-start.42 = (bf16[2,9,256]{2,1,0:T(8,128)(2,1)S(1)}, bf16[2,9,256]{2,1,0:T(8,128)(2,1)}, u32[]{:S(2)}) copy-start(bf16[2,9,256]{2,1,0:T(8,128)(2,1)} %copy.141) | copy-start | bytes 27652
  484.4 62.7 %all-to-all-start.7 = ((bf16[8,2,192,256]{3,2,1,0:T(8,128)(2,1)}), bf16[8,2,192,256]{3,2,1,0:T(8,128)(2,1)S(1)}, u32[]{:S(2)}, u32[]{:S(2)}) async-start(bf16[8,2,192,256]{3,2,1,0:T(8,128)(2,1)} %get-tuple-element.10), calls=%async_computation.7 | async-start | bytes 3145728 | tf_op jit(solution)/shard_map/all_to_all | solution.py:29
  508.1 3.3 copy-start.35
  508.1 3.3 copy-start.61
  547.1 57.1 %all-to-all-start.10 = ((bf16[32,80,768]{2,1,0:T(8,128)(2,1)}), bf16[32,80,768]{2,1,0:T(8,128)(2,1)}, u32[]{:S(2)}, u32[]{:S(2)}) async-start(bf16[32,80,768]{2,1,0:T(8,128)(2,1)} %concatenate.35), calls=%async_computation.10 | async-start | bytes 7864320 | tf_op jit(solution)/shard_map/all_to_all | solution.py:29
  555.9 2.0 copy-start.6
  557.9 7.0 %copy-start.4 = (bf16[2,256,768]{2,1,0:T(8,128)(2,1)S(1)}, bf16[2,256,768]{2,1,0:T(8,128)(2,1)}, u32[]{:S(2)}) copy-start(bf16[2,256,768]{2,1,0:T(8,128)(2,1)} %copy-done.2) | copy-start | bytes 2359300
  557.9 7.0 %copy-start.30 = (bf16[2,192,256]{2,1,0:T(8,128)(2,1)S(1)}, bf16[2,192,256]{2,1,0:T(8,128)(2,1)}, u32[]{:S(2)}) copy-start(bf16[2,192,256]{2,1,0:T(8,128)(2,1)} %copy-done.29) | copy-start | bytes 589828
  557.9 7.0 %copy-start.32 = (bf16[2,3,2,32,256]{4,3,2,1,0:T(8,128)(2,1)S(1)}, bf16[2,3,2,32,256]{4,3,2,1,0:T(8,128)(2,1)}, u32[]{:S(2)}) copy-start(bf16[2,3,2,32,256]{4,3,2,1,0:T(8,128)(2,1)} %copy-done.31) | copy-start | bytes 589828
  557.9 7.0 %copy-start.34 = (bf16[2,3,2,32,256]{4,3,2,1,0:T(8,128)(2,1)S(1)}, bf16[2,3,2,32,256]{4,3,2,1,0:T(8,128)(2,1)}, u32[]{:S(2)}) copy-start(bf16[2,3,2,32,256]{4,3,2,1,0:T(8,128)(2,1)} %copy-done.33) | copy-start | bytes 589828
  560.8 6.1 collective-permute-start.5
  568.9 40.6 %copy-start.59 = (s32[3]{0:T(128)S(1)}, s32[3]{0:T(128)}, u32[]{:S(2)}) copy-start(s32[3]{0:T(128)} %fusion.59) | copy-start | bytes 40
  568.9 40.6 %copy-start.14 = (f32[2,64,768]{2,1,0:T(8,128)S(1)}, f32[2,64,768]{2,1,0:T(8,128)}, u32[]{:S(2)}) copy-start(f32[2,64,768]{2,1,0:T(8,128)} %copy-done.13) | copy-start | bytes 1179652
  568.9 40.6 %copy-start.46 = (f32[2,64]{1,0:T(2,128)S(1)}, f32[2,64]{1,0:T(2,128)}, u32[]{:S(2)}) copy-start(f32[2,64]{1,0:T(2,128)} %copy-done.45) | copy-start | bytes 1540
  568.9 40.6 %copy-start.49 = (f32[2,64]{1,0:T(2,128)S(1)}, f32[2,64]{1,0:T(2,128)}, u32[]{:S(2)}) copy-start(f32[2,64]{1,0:T(2,128)} %copy-done.48) | copy-start | bytes 1540
  568.9 40.6 %copy-start.56 = (f32[2,64]{1,0:T(2,128)S(1)}, f32[2,64]{1,0:T(2,128)}, u32[]{:S(2)}) copy-start(f32[2,64]{1,0:T(2,128)} %copy-done.55) | copy-start | bytes 1540
  569.0 40.6 %copy-start.18 = (f32[2,2,64,768]{3,2,0,1:T(8,128)S(1)}, f32[2,2,64,768]{3,2,0,1:T(8,128)}, u32[]{:S(2)}) copy-start(f32[2,2,64,768]{3,2,0,1:T(8,128)} %copy-done.17) | copy-start | bytes 2359300
  569.0 40.5 %collective-permute-start.6 = (bf16[2,64,768]{2,1,0:T(8,128)(2,1)S(1)}, bf16[2,64,768]{2,1,0:T(8,128)(2,1)S(1)}, u32[]{:S(2)}, u32[]{:S(2)}) collective-permute-start(bf16[2,64,768]{2,1,0:T(8,128)(2,1)S(1)} %fusion.37), channel_id=1, source_target_pairs={{0,2},{2,0},{1,3},{3,1},{4,6},{6,4},{5,7},{7,5},{8,10},{10,8},{9,1... | collective-permute-start | bytes 589832 | tf_op jit(solution)/shard_map/ppermute | solution.py:37
  604.2 19.2 %all-to-all-start.9 = ((bf16[32,24,576]{2,1,0:T(8,128)(2,1)}), bf16[32,24,576]{2,1,0:T(8,128)(2,1)S(1)}, u32[]{:S(2)}, u32[]{:S(2)}) async-start(bf16[32,24,576]{2,1,0:T(8,128)(2,1)} %bitcast.57), calls=%async_computation.9 | async-start | bytes 1966080 | tf_op jit(solution)/shard_map/all_to_all | solution.py:29
  613.1 28.3 %copy-start.57 = (pred[3]{0:T(512)(128)(4,1)S(1)}, pred[3]{0:T(512)(128)(4,1)}, u32[]{:S(2)}) copy-start(pred[3]{0:T(512)(128)(4,1)} %compare_and_fusion) | copy-start | bytes 13
  613.4 25.5 %collective-permute-start.7 = (bf16[96,192]{1,0:T(8,128)(2,1)S(1)}, bf16[96,192]{1,0:T(8,128)(2,1)S(1)}, u32[]{:S(2)}, u32[]{:S(2)}) collective-permute-start(bf16[96,192]{1,0:T(8,128)(2,1)S(1)} %convert_element_type.240), channel_id=1, source_target_pairs={{0,0},{1,32},{2,64},{3,96},{32,1},{33,33},{34,65},{35,97},{64,2},{... | collective-permute-start | bytes 110600 | tf_op jit(solution)/shard_map/ppermute | solution.py:415
  624.5 16.3 %all-to-all-start.11 = ((bf16[4,32,192]{2,1,0:T(8,128)(2,1)}), bf16[4,32,192]{2,1,0:T(8,128)(2,1)S(1)}, u32[]{:S(2)}, u32[]{:S(2)}) async-start(bf16[4,32,192]{2,1,0:T(8,128)(2,1)} %copy.158), calls=%async_computation.11 | async-start | bytes 131072 | tf_op jit(solution)/shard_map/all_to_all | solution.py:29
  (16 other events, 15.3 us)

commit v2 on v1

--- a/solution.py
+++ b/solution.py
@@ -19,6 +19,7 @@
 KAX = ("y",)
 NQ = 8
 NK = 4
+STEP = 4
 LOG2E = math.log2(math.e)
 NEG = -1e30
 f32 = jnp.float32
@@ -93,129 +94,112 @@
     return n
 
 
-def attend_kernel(lens_ref, start_ref, q_ref, kv_ref, out_ref, kx_ref, vx_ref, o_ref, m_ref):
+def pick_tiles(lens_ref, start_ref, seq, run):
+    n = valid_tiles(lens_ref, start_ref, seq)
+    for tiles in range(1, NK + 1):
+        pl.when(n == tiles)(functools.partial(run, seq, tiles))
+
+
+def attend_kernel(lens_ref, start_ref, q_ref, kv_ref, out_ref, kx_ref, vx_ref, sum_ref, peak_ref):
     row = lax.broadcasted_iota(jnp.int32, (16, 256), 0)
     one_row = jnp.where(row == 0, 1.0, 0.0).astype(bf16)
+    one_rows = jnp.concatenate([one_row] * STEP, 1)
     for seq in range(2):
         for tile in range(NK):
             extra = key_bias(lens_ref, start_ref, seq, tile)
+            here = pl.ds(256 * tile, 256)
             for h in range(3):
                 kt = jnp.concatenate([kv_ref[tile, seq, pl.ds(64 * h, 64), :], extra], 0)
-                kx_ref[tile, seq, h] = jnp.transpose(kt)
-                vx_ref[tile, seq, h, pl.ds(0, 64), :] = kv_ref[tile, seq, pl.ds(192 + 64 * h, 64), :]
-                vx_ref[tile, seq, h, pl.ds(64, 16), :] = one_row
-    for seq in range(2):
-        tiles = valid_tiles(lens_ref, start_ref, seq)
-
-        @pl.loop(0, NQ)
-        def _(block):
-            qx = [
-                jnp.concatenate([q_ref[block, seq, pl.ds(64 * h, 64), :], one_row], 0)
-                for h in range(3)
-            ]
-
-            def step(tile, first):
-                for h in range(3):
-                    s = jnp.dot(kx_ref[tile, seq, h], qx[h], preferred_element_type=f32)
-                    peak = jnp.max(s, 0, keepdims=True)
-                    if not first:
-                        before = m_ref[h, pl.ds(0, 1), :]
-                        peak = jnp.maximum(before, peak)
-                    p = jnp.exp2(s - peak).astype(bf16)
-                    o = jnp.dot(vx_ref[tile, seq, h], p, preferred_element_type=f32)
-                    if not first:
-                        o = o + o_ref[h] * jnp.exp2(before - peak)
-                    o_ref[h] = o
-                    m_ref[h, pl.ds(0, 1), :] = peak
-
-            step(0, True)
-
-            @pl.loop(1, tiles)
-            def _(tile):
-                step(tile, False)
-
-            rows = []
+                kx_ref[seq, h, here, :] = jnp.transpose(kt)
+                vx_ref[seq, h, pl.ds(0, 64), here] = kv_ref[tile, seq, pl.ds(192 + 64 * h, 64), :]
+                vx_ref[seq, h, pl.ds(64, 16), here] = one_row
+
+    def run(seq, tiles):
+        keys = pl.ds(0, 256 * tiles)
+
+        @pl.loop(0, NQ // STEP)
+        def _(turn):
             for h in range(3):
-                total = o_ref[h, pl.ds(64, 1), :]
-                out_ref[block, seq, pl.ds(64 * h, 64), :] = (
-                    o_ref[h, pl.ds(0, 64), :] / total
-                ).astype(bf16)
-                lse = m_ref[h, pl.ds(0, 1), :] + jnp.log2(total)
-                rows += [part.astype(f32) for part in split3(lse)]
-            rows.append(jnp.zeros((7, 256), f32))
+                q = [q_ref[turn * STEP + j, seq, pl.ds(64 * h, 64), :] for j in range(STEP)]
+                qx = jnp.concatenate([jnp.concatenate(q, 1), one_rows], 0)
+                s = jnp.dot(kx_ref[seq, h, keys, :], qx, preferred_element_type=f32)
+                peak = jnp.max(s, 0, keepdims=True)
+                p = jnp.exp2(s - peak).astype(bf16)
+                o = jnp.dot(vx_ref[seq, h, :, keys], p, preferred_element_type=f32)
+                total = o[64:65]
+                o = (o[:64] * (1.0 / total)).astype(bf16)
+                for j in range(STEP):
+                    here = slice(256 * j, 256 * j + 256)
+                    out_ref[turn * STEP + j, seq, pl.ds(64 * h, 64), :] = o[:, here]
+                    sum_ref[turn * STEP + j, seq, pl.ds(h, 1), :] = total[:, here]
+                    peak_ref[turn * STEP + j, seq, pl.ds(h, 1), :] = peak[:, here]
+
+    for seq in range(2):
+        pick_tiles(lens_ref, start_ref, seq, run)
+    for seq in range(2):
+        for block in range(NQ):
+            lse = peak_ref[block, seq, pl.ds(0, 3), :] + jnp.log2(sum_ref[block, seq, pl.ds(0, 3), :])
+            rows = [part.astype(f32) for part in split3(lse)] + [jnp.zeros((7, 256), f32)]
             out_ref[block, seq, pl.ds(192, 16), :] = jnp.concatenate(rows, 0).astype(bf16)
 
 
 def attend_back_kernel(
-    lens_ref, start_ref, q_ref, kv_ref, g_ref, dq_ref, dkv_ref, kx_ref, vx_ref, dk_ref, dv_ref, acc_ref
+    lens_ref, start_ref, q_ref, kv_ref, g_ref, dq_ref, dkv_ref, kx_ref, vx_ref, kt_ref, dk_ref, dv_ref
 ):
     row = lax.broadcasted_iota(jnp.int32, (16, 256), 0)
     ones = jnp.where(row < 3, 1.0, 0.0).astype(bf16)
+    one = jnp.ones((1, 256), f32)
+    nt = (((1,), (1,)), ((), ()))
     for seq in range(2):
         for tile in range(NK):
             extra = key_bias(lens_ref, start_ref, seq, tile)
+            here = pl.ds(256 * tile, 256)
             for h in range(3):
-                kt = jnp.concatenate([kv_ref[tile, seq, pl.ds(64 * h, 64), :], extra], 0)
-                kx_ref[tile, seq, h] = jnp.transpose(kt)
-                vt = jnp.concatenate([kv_ref[tile, seq, pl.ds(192 + 64 * h, 64), :], ones], 0)
-                vx_ref[tile, seq, h] = jnp.transpose(vt)
+                k = kv_ref[tile, seq, pl.ds(64 * h, 64), :]
+                v = kv_ref[tile, seq, pl.ds(192 + 64 * h, 64), :]
+                kx_ref[seq, h, here, :] = jnp.transpose(jnp.concatenate([k, extra], 0))
+                vx_ref[seq, h, here, :] = jnp.transpose(jnp.concatenate([v, ones], 0))
+                kt_ref[seq, h, :, here] = k
     dk_ref[...] = jnp.zeros_like(dk_ref)
     dv_ref[...] = jnp.zeros_like(dv_ref)
-    nt = (((1,), (1,)), ((), ()))
-    for seq in range(2):
-        tiles = valid_tiles(lens_ref, start_ref, seq)
+
+    def run(seq, tiles):
+        keys = pl.ds(0, 256 * tiles)
 
         @pl.loop(0, NQ)
         def _(block):
             stats = g_ref[block, seq, pl.ds(192, 32), :].astype(f32)
-            one = jnp.ones((1, 256), f32)
-            q, g, qx, gx = [], [], [], []
             for h in range(3):
-                q.append(q_ref[block, seq, pl.ds(64 * h, 64), :])
-                g.append(g_ref[block, seq, pl.ds(64 * h, 64), :])
-                extra = jnp.concatenate(
-                    [one, stats[3 * h : 3 * h + 3], jnp.zeros((12, 256), f32)], 0
-                ).astype(bf16)
-                qx.append(jnp.concatenate([q[h], extra], 0))
-                extra = jnp.concatenate(
-                    [stats[16 + 3 * h : 16 + 3 * h + 3], jnp.zeros((13, 256), f32)], 0
-                ).astype(bf16)
-                gx.append(jnp.concatenate([g[h], extra], 0))
-
-            acc_ref[...] = jnp.zeros_like(acc_ref)
-
-            @pl.loop(0, tiles)
-            def _(tile):
-                for h in range(3):
-                    s = jnp.dot(kx_ref[tile, seq, h], qx[h], preferred_element_type=f32)
-                    p = jnp.exp2(s)
-                    d = jnp.dot(vx_ref[tile, seq, h], gx[h], preferred_element_type=f32)
-                    ds = (p * d).astype(bf16)
-                    acc_ref[h] += jnp.dot(
-                        kv_ref[tile, seq, pl.ds(64 * h, 64), :], ds, preferred_element_type=f32
-                    )
-                    dk_ref[tile, seq, h] += lax.dot_general(
-                        q[h], ds, nt, preferred_element_type=f32
-                    )
-                    dv_ref[tile, seq, h] += lax.dot_general(
-                        g[h], p.astype(bf16), nt, preferred_element_type=f32
-                    )
-
+                q = q_ref[block, seq, pl.ds(64 * h, 64), :]
+                g = g_ref[block, seq, pl.ds(64 * h, 64), :]
+                rows = [one, stats[3 * h : 3 * h + 3], jnp.zeros((12, 256), f32)]
+                qx = jnp.concatenate([q, jnp.concatenate(rows, 0).astype(bf16)], 0)
+                rows = [stats[16 + 3 * h : 16 + 3 * h + 3], jnp.zeros((13, 256), f32)]
+                gx = jnp.concatenate([g, jnp.concatenate(rows, 0).astype(bf16)], 0)
+                p = jnp.exp2(jnp.dot(kx_ref[seq, h, keys, :], qx, preferred_element_type=f32))
+                d = jnp.dot(vx_ref[seq, h, keys, :], gx, preferred_element_type=f32)
+                ds = (p * d).astype(bf16)
+                dq = jnp.dot(kt_ref[seq, h, :, keys], ds, preferred_element_type=f32)
+                dk_ref[seq, h, :, keys] += lax.dot_general(q, ds, nt, preferred_element_type=f32)
+                dv_ref[seq, h, :, keys] += lax.dot_general(
+                    g, p.astype(bf16), nt, preferred_element_type=f32
+                )
+                dq_ref[block, seq, pl.ds(64 * h, 64), :] = (dq * HEAD**-0.5).astype(bf16)
+
+    for seq in range(2):
+        pick_tiles(lens_ref, start_ref, seq, run)
+    for seq in range(2):
+        for tile in range(NK):
+            here = pl.ds(256 * tile, 256)
             for h in range(3):
-                dq_ref[block, seq, pl.ds(64 * h, 64), :] = (acc_ref[h] * HEAD**-0.5).astype(bf16)
-
-    for seq in range(2):
-        for tile in range(NK):
-            for h in range(3):
-                dkv_ref[tile, seq, pl.ds(64 * h, 64), :] = (
-                    dk_ref[tile, seq, h] * (1.0 / LOG2E)
-                ).astype(bf16)
-                dkv_ref[tile, seq, pl.ds(192 + 64 * h, 64), :] = dv_ref[tile, seq, h].astype(bf16)
+                dk = dk_ref[seq, h, :, here] * (1.0 / LOG2E)
+                dkv_ref[tile, seq, pl.ds(64 * h, 64), :] = dk.astype(bf16)
+                dkv_ref[tile, seq, pl.ds(192 + 64 * h, 64), :] = dv_ref[seq, h, :, here].astype(bf16)
 
 
 SMEM = pl.BlockSpec(memory_space=pltpu.SMEM)
 VMEM = pl.BlockSpec(memory_space=pltpu.VMEM)
-PARAMS = pltpu.CompilerParams(vmem_limit_bytes=48 * 1024 * 1024)
+PARAMS = pltpu.CompilerParams(vmem_limit_bytes=56 * 1024 * 1024)
 
 
 def attend(lengths, starts, q_all, kv_all):
@@ -225,14 +209,14 @@
         in_specs=[SMEM, SMEM, VMEM, VMEM],
         out_specs=VMEM,
         scratch_shapes=[
-            pltpu.VMEM((NK, 2, 3, 256, 80), bf16),
-            pltpu.VMEM((NK, 2, 3, 80, 256), bf16),
-            pltpu.VMEM((3, 80, 256), f32),
-            pltpu.VMEM((3, 8, 256), f32),
+            pltpu.VMEM((2, 3, 1024, 80), bf16),
+            pltpu.VMEM((2, 3, 80, 1024), bf16),
+            pltpu.VMEM((NQ, 2, 8, 256), f32),
+            pltpu.VMEM((NQ, 2, 8, 256), f32),
         ],
         compiler_params=PARAMS,
         cost_estimate=pl.CostEstimate(
-            flops=12_582_912 * 512, bytes_accessed=5_000_000, transcendentals=12_582_912
+            flops=23_000_000_000, bytes_accessed=5_000_000, transcendentals=12_582_912
         ),
     )(lengths, starts, q_all, kv_all)
 
@@ -247,15 +231,15 @@
         in_specs=[SMEM, SMEM, VMEM, VMEM, VMEM],
         out_specs=(VMEM, VMEM),
         scratch_shapes=[
-            pltpu.VMEM((NK, 2, 3, 256, 80), bf16),
-            pltpu.VMEM((NK, 2, 3, 256, 80), bf16),
-            pltpu.VMEM((NK, 2, 3, 64, 256), f32),
-            pltpu.VMEM((NK, 2, 3, 64, 256), f32),
-            pltpu.VMEM((3, 64, 256), f32),
+            pltpu.VMEM((2, 3, 1024, 80), bf16),
+            pltpu.VMEM((2, 3, 1024, 80), bf16),
+            pltpu.VMEM((2, 3, 64, 1024), bf16),
+            pltpu.VMEM((2, 3, 64, 1024), f32),
+            pltpu.VMEM((2, 3, 64, 1024), f32),
         ],
         compiler_params=PARAMS,
         cost_estimate=pl.CostEstimate(
-            flops=12_582_912 * 1280, bytes_accessed=8_000_000, transcendentals=12_582_912
+            flops=46_000_000_000, bytes_accessed=8_000_000, transcendentals=12_582_912
         ),
     )(lengths, starts, q_all, kv_all, g_all)
 
@@ -268,24 +252,28 @@
     slots = own_slots * 4
 
     blocks = w_qkv.reshape(24, 3, 192).transpose(1, 0, 2)
-    picks = (jnp.arange(4) - 3 * n_i) % 4
-    sent = jnp.take(blocks, jnp.minimum(picks, 2), axis=0)
+    picks = jnp.minimum((jnp.arange(4) - 3 * n_i) % 4, 2)
+    norm_row = jnp.pad(norm_params, ((0, 7), (0, 168)))
+    sent = jnp.concatenate(
+        [
+            jnp.take(blocks, picks, axis=0),
+            jnp.broadcast_to(jnp.concatenate([w_out, norm_row])[None], (4, 32, 192)),
+        ],
+        axis=1,
+    )
     got = exchange(sent, NARROW)
     sources = (4 * jnp.arange(3) + n_i) // 3
-    qkv_mine = jnp.take(got, sources, axis=0).transpose(1, 0, 2).reshape(24, 576)
+    qkv_mine = jnp.take(got[:, :24], sources, axis=0).transpose(1, 0, 2).reshape(24, 576)
     wqkv = gather(qkv_mine, WIDE, 32).reshape(width, 576)
 
-    turn_pairs = [
-        ((y * 4 + n), (n * 4 + y)) for y in range(4) for n in range(4)
-    ]
+    turn_pairs = [((y * 4 + n), (n * 4 + y)) for y in range(4) for n in range(4)]
     down_turned = lax.ppermute(w_down, ("y",) + NARROW, turn_pairs)
-    out_rows = narrow_gather(w_out)
-    norm_rows = lax.all_gather(norm_params, NARROW, axis=0, tiled=True)
-    norm_row = jnp.pad(norm_rows.reshape(1, 96), ((0, 7), (0, width - 96)))
+    out_rows = got[:, 24:48].transpose(1, 0, 2).reshape(24, width)
+    norm_row = jnp.pad(got[:, 48, :24].reshape(1, 96), ((0, 7), (0, width - 96)))
     packed = jnp.concatenate(
         [w_gate, w_up, out_rows, down_turned.reshape(24, width), norm_row], axis=0
     )
-    all_weights = gather(packed, WIDE, 32)
+    all_weights = lax.all_gather(packed, WIDE)
     wgate = all_weights[:, 0:24].reshape(width, width)
     wup = all_weights[:, 24:48].reshape(width, width)
     wout = all_weights[:, 48:72].reshape(width, width)
@@ -319,7 +307,7 @@
     starts = (jnp.arange(NK) * 8 + z_i * 2 + xh_i).astype(jnp.int32) * slots
     parts = attend(lengths, starts, q_all, kv_all)
     parts = exchange(parts, QAX).astype(f32)
-    part_lse = jnp.sum(parts[:, :, 192:201].reshape(NQ, seqs, 3, 3, slots), 3)
+    part_lse = jnp.sum(parts[:, :, 192:201].reshape(NQ, seqs, 3, 3, slots), 2)
     top = jnp.max(part_lse, 0)
     lse = top + jnp.log2(jnp.sum(jnp.exp2(part_lse - top), 0))
     shares = jnp.exp2(part_lse - lse)
@@ -394,31 +382,33 @@
     )
     g_all = gather(sent_back, QAX, NQ)
 
-    res_cols = lax.dynamic_slice_in_dim(res_low, n_i * 192, 192, 2)
-    grad_wout = jnp.einsum("sft,std->fd", attn_all, res_cols, preferred_element_type=f32)
     grad_norm_rows = jnp.stack([grad_gain1, grad_bias1, grad_gain2, grad_bias2])
     norm_blocks = grad_norm_rows.reshape(4, 32, 24).transpose(1, 0, 2).reshape(32, 1, 96)
-    norm_blocks = jnp.pad(norm_blocks, ((0, 0), (0, 1), (0, width - 96)))
+    norm_blocks = jnp.pad(norm_blocks, ((0, 0), (0, 7), (0, width - 96))).astype(bf16)
     grads_packed = jnp.concatenate(
         [
-            grad_wgate.reshape(32, 24, width),
-            grad_wup.reshape(32, 24, width),
-            grad_wdown.reshape(8, 96, 4, 192).transpose(2, 0, 1, 3).reshape(32, 24, width),
-            grad_wout.reshape(32, 6, width),
+            grad_wgate.astype(bf16).reshape(32, 24, width),
+            grad_wup.astype(bf16).reshape(32, 24, width),
+            grad_wdown.astype(bf16)
+            .reshape(8, 96, 4, 192)
+            .transpose(2, 0, 1, 3)
+            .reshape(32, 24, width),
             norm_blocks,
         ],
         axis=1,
-    ).astype(bf16)
-    grads_got = jnp.sum(exchange(grads_packed, WIDE).astype(f32), 0)
+    )
+    grads_packed, g_all = lax.optimization_barrier((grads_packed, g_all))
+    grads_got = exchange(grads_packed, WIDE)
+    dq_parts, dkv_parts = attend_back(lengths, starts, q_all, kv_all, g_all)
+    grads_got, dq_parts, dkv_parts = lax.optimization_barrier((grads_got, dq_parts, dkv_parts))
+    grads_got = jnp.sum(grads_got.astype(f32), 0)
     sum_gate = grads_got[0:24]
     sum_up = grads_got[24:48]
     sum_down = lax.ppermute(
         grads_got[48:72].reshape(96, 192).astype(bf16), ("y",) + NARROW, turn_pairs
     ).astype(f32)
-    sum_out = grads_got[72:78].reshape(24, 192)
-    norm_sums = grads_got[78, :96].reshape(4, 24)
-
-    dq_parts, dkv_parts = attend_back(lengths, starts, q_all, kv_all, g_all)
+    norm_sums = grads_got[72, :96].reshape(4, 24)
+
     grad_query = jnp.sum(exchange(dq_parts, QAX).astype(f32), 0)
     grad_keyval = jnp.sum(exchange(dkv_parts, KAX).astype(f32), 0)
 
@@ -435,10 +425,12 @@
     grad_wqkv = jnp.einsum("std,sft->df", tokens, grad_proj, preferred_element_type=f32)
     input_part = jnp.einsum("sft,df->std", grad_proj, wqkv, preferred_element_type=f32)
     grad_input = (grad_first + sum_to_own(input_part)).astype(bf16)
-    qkv_got = jnp.sum(
-        exchange(grad_wqkv.reshape(32, 24, 576).astype(bf16), WIDE).astype(f32), 0
-    )
-    back = qkv_got.reshape(24, 3, 192).transpose(1, 0, 2)
+    res_cols = lax.dynamic_slice_in_dim(res_low, n_i * 192, 192, 2)
+    grad_wout = jnp.einsum("sft,std->fd", attn_all, res_cols, preferred_element_type=f32)
+    last = jnp.concatenate([grad_wqkv.astype(bf16), grad_wout.astype(bf16)], axis=1)
+    last_got = jnp.sum(exchange(last.reshape(32, 24, width), WIDE).astype(f32), 0)
+    sum_out = last_got[:, 576:]
+    back = last_got[:, :576].reshape(24, 3, 192).transpose(1, 0, 2)
     where = (sources[None, :] == jnp.arange(4)[:, None]).astype(f32)
     back_sent = jnp.einsum("sk,kdf->sdf", where, back)
     norm_sent = jnp.pad(norm_sums[:, None, :], ((0, 0), (0, 7), (0, 168)))

time: 637 us -> 466 us (0.73); the launches traced: 643 us -> 457 us
  blocking collectives: 177 us -> 69.4 us
  Pallas kernels: 129 us -> 49.6 us
  waiting for transfers between devices: 97 us -> 143 us
  local copies, waits for them, and re-layouts: 90.3 us -> 50.7 us
  starting transfers between devices: 97.1 us -> 77.1 us
  between operations: 2.32 us -> 15.7 us
    all_gather x5 -> x4, blocking collectives: 118 us -> 47.5 us  [narrow_gather(): return lax.all_gather(x, NARROW, axis=1, tiled=True)]
    pallas_call x1, Pallas kernels: 59.4 us -> 16.7 us  [attend(): pl.pallas_call(attend_kernel, out_shape=jax.ShapeDtypeStruct((NQ, 2, 208,...]
    all_to_all x10, waiting for transfers between devices: 86.9 us -> 127 us  [exchange(): return lax.all_to_all(x, axes, 0, 0, tiled=True)]
    pallas_call x1, Pallas kernels: 69.8 us -> 33 us  [attend_back(): pl.pallas_call(attend_back_kernel, out_shape=(jax.ShapeDtypeStruct((NQ, 2...]
    all_to_all x2 -> x1, blocking collectives: 53.9 us -> 21.9 us  [exchange(): return lax.all_to_all(x, axes, 0, 0, tiled=True)]
    concatenate x1, local copies, waits for them, and re-layouts: 20.2 us -> 1.46 us  [on_device(): jnp.concatenate([grad_wqkv.astype(bf16), grad_wout.astype(bf16)], axis=1)]
    all_to_all x10, starting transfers between devices: 71.1 us -> 58.7 us  [exchange(): return lax.all_to_all(x, axes, 0, 0, tiled=True)]
  transfers between devices with their start and end apart: 18 -> 19, of which waited for: 11 -> 13; matrix products, arithmetic and copies ran while one was open for 13% -> 11% of each run, Pallas kernels for 0% -> 11%
where the time goes in v2:
time: 466 us; the launch traced here: 457 us
  waiting for transfers between devices  143 us (31%)
  starting transfers between devices  77.1 us (17%)
  blocking collectives  69.4 us (15%)
  local copies, waits for them, and re-layouts  50.7 us (11%)
  Pallas kernels  49.6 us (11%)
  other arithmetic  27.2 us (6%)
  matrix products  23.5 us (5%)
  between operations  15.7 us (3%)
    all_to_all x10, waiting for transfers between devices, exchange(): return lax.all_to_all(x, axes, 0, 0, tiled=True)  127 us
    all_to_all x10, starting transfers between devices, exchange(): return lax.all_to_all(x, axes, 0, 0, tiled=True)  58.7 us
    all_gather x4, blocking collectives, narrow_gather(): return lax.all_gather(x, NARROW, axis=1, tiled=True)  47.5 us
    pallas_call x1, Pallas kernels, attend_back(): pl.pallas_call(attend_back_kernel, out_shape=(jax.ShapeDtypeStruct((NQ, 2...  33 us
    all_to_all x1, blocking collectives, exchange(): return lax.all_to_all(x, axes, 0, 0, tiled=True)  21.9 us
    pallas_call x1, Pallas kernels, attend(): pl.pallas_call(attend_kernel, out_shape=jax.ShapeDtypeStruct((NQ, 2, 208,...  16.7 us
    ppermute x6, waiting for transfers between devices, flip(): return lax.ppermute(x, axis, [(0, 1), (1, 0)])  13 us
    ppermute x6, starting transfers between devices, flip(): return lax.ppermute(x, axis, [(0, 1), (1, 0)])  11.9 us
  transfers between devices with their start and end apart: 19, of which 13 were waited for; matrix products, arithmetic and copies ran while one was open for 11% of the time, Pallas kernels for 11%

profile of v2, /device:TPU:1, one launch (start us, length us, event | category | flops | bytes accessed | tf_op | source)
XLA Modules:
  0.0 456.5 jit_solution(5870623098441052524)
XLA Ops:
  10.1 4.7 %all-to-all-start = ((bf16[4,56,192]{2,1,0:T(8,128)(2,1)}), bf16[4,56,192]{2,1,0:T(8,128)(2,1)S(1)}, u32[]{:S(2)}, u32[]{:S(2)}) async-start(bf16[4,56,192]{2,1,0:T(8,128)(2,1)} %pad_maximum_fusion.7), calls=%async_computation | async-start | bytes 229376 | tf_op jit(solution)/shard_map/all_to_all | solution.py:30
  14.8 3.3 collective-permute-start
  22.4 1.1 broadcast_in_dim.47
  23.5 12.6 %all-to-all-start.1 = ((bf16[32,24,576]{2,1,0:T(8,128)(2,1)}), bf16[32,24,576]{2,1,0:T(8,128)(2,1)S(1)}, u32[]{:S(2)}, u32[]{:S(2)}) async-start(bf16[32,24,576]{2,1,0:T(8,128)(2,1)} %broadcast_in_dim.47), calls=%async_computation.1 | async-start | bytes 1966080 | tf_op jit(solution)/shard_map/all_to_all | solution.py:30
  36.4 17.0 %all_gather.18 = bf16[2,256,768]{2,1,0:T(8,128)(2,1)S(1)} all-gather(bf16[2,64,768]{2,1,0:T(8,128)(2,1)S(1)} %copy-done.25), channel_id=1, replica_groups=mesh['y'=4,'z'=4,'xh'=2,'xl'=2,'c'=2] {'xl','c'}, dimensions={1}, use_global_device_ids=true | all-gather | bytes 983040 | tf_op jit(solution)/shard_map/all_gather | solution.py:72
  53.4 1.4 all-to-all-done.1
  55.9 1.3 broadcast_in_dim.49
  57.3 3.6 all-to-all-start.3
  60.9 22.0 %all-to-all-done.3.kv_ref = bf16[4,2,384,256]{3,2,1,0:T(8,128)(2,1)S(1)} async-done(((bf16[4,2,384,256]{3,2,1,0:T(8,128)(2,1)}), bf16[4,2,384,256]{3,2,1,0:T(8,128)(2,1)S(1)}, u32[]{:S(2)}, u32[]{:S(2)}) %all-to-all-start.3) | async-done | bytes 1572896 | tf_op jit(solution)/shard_map/all_to_all | solution.py:30
  82.9 1.5 broadcast_in_dim.48
  84.6 8.0 %all-to-all-start.2 = ((bf16[8,2,192,256]{3,2,1,0:T(8,128)(2,1)}), bf16[8,2,192,256]{3,2,1,0:T(8,128)(2,1)}, u32[]{:S(2)}, u32[]{:S(2)}) async-start(bf16[8,2,192,256]{3,2,1,0:T(8,128)(2,1)} %broadcast_in_dim.48), calls=%async_computation.2 | async-start | bytes 3145728 | tf_op jit(solution)/shard_map/all_to_all | solution.py:30
  93.1 38.7 %all-to-all-done.2.q_ref = bf16[8,2,192,256]{3,2,1,0:T(8,128)(2,1)} async-done(((bf16[8,2,192,256]{3,2,1,0:T(8,128)(2,1)}), bf16[8,2,192,256]{3,2,1,0:T(8,128)(2,1)}, u32[]{:S(2)}, u32[]{:S(2)}) %all-to-all-start.2) | async-done | bytes 1572896 | tf_op jit(solution)/shard_map/all_to_all | solution.py:30
  131.8 16.7 %shard_map.152 = bf16[8,2,208,256]{3,2,1,0:T(8,128)(2,1)} custom-call(s32[2]{0:T(128)} %lens_ref.3, s32[4]{0:T(128)} %add_multiply_fusion.start_ref, bf16[8,2,192,256]{3,2,1,0:T(8,128)(2,1)} %all-to-all-done.2.q_ref, bf16[4,2,384,256]{3,2,1,0:T(8,128)(2,1)} %copy-done.13), custom_call_target="tpu_custom_call" | custom-call | flops 23000000512 | bytes 5000000 | tf_op jit(solution)/shard_map/pallas_call | solution.py:206
  148.5 3.7 all-to-all-start.4
  152.9 21.2 %all-to-all-done.4 = bf16[8,2,208,256]{3,2,1,0:T(8,128)(2,1)S(1)} async-done(((bf16[8,2,208,256]{3,2,1,0:T(8,128)(2,1)}), bf16[8,2,208,256]{3,2,1,0:T(8,128)(2,1)S(1)}, u32[]{:S(2)}, u32[]{:S(2)}) %all-to-all-start.4) | async-done | bytes 1703968 | tf_op jit(solution)/shard_map/all_to_all | solution.py:30
  176.4 12.3 %all_gather.19 = bf16[2,768,256]{2,1,0:T(8,128)(2,1)S(1)} all-gather(bf16[2,192,256]{2,1,0:T(8,128)(2,1)S(1)} %convert_element_type.203), channel_id=1, replica_groups=mesh['y'=4,'z'=4,'xh'=2,'xl'=2,'c'=2] {'xl','c'}, dimensions={1}, use_global_device_ids=true | all-gather | bytes 983040 | tf_op jit(solution)/shard_map/all_gather | solution.py:72
  189.5 4.3 fusion.62
  194.8 2.4 reshape.612
  197.2 2.6 copy.152
  199.9 2.2 reshape.657
  202.1 2.2 fusion.9
  207.3 2.0 multiply_convert_fusion.2
  211.0 1.1 copy-done.19
  212.9 2.2 reshape.613
  216.9 1.2 bitcast_add_fusion.2
  218.3 6.1 %collective-permute-done.2 = bf16[2,64,768]{2,1,0:T(8,128)(2,1)S(1)} collective-permute-done((bf16[2,64,768]{2,1,0:T(8,128)(2,1)S(1)}, bf16[2,64,768]{2,1,0:T(8,128)(2,1)S(1)}, u32[]{:S(2)}, u32[]{:S(2)}) %collective-permute-start.2) | collective-permute-done | bytes 196640 | tf_op jit(solution)/shard_map/ppermute | solution.py:38
  225.9 8.9 %all_gather.22 = bf16[2,256,768]{2,1,0:T(8,128)(2,1)S(1)} all-gather(bf16[2,64,768]{2,1,0:T(8,128)(2,1)S(1)} %fusion.34), channel_id=1, replica_groups=mesh['y'=4,'z'=4,'xh'=2,'xl'=2,'c'=2] {'xl','c'}, dimensions={1}, use_global_device_ids=true | all-gather | bytes 983040 | tf_op jit(solution)/shard_map/all_gather | solution.py:72
  234.8 1.2 multiply_convert_fusion
  239.7 1.9 collective-permute-done.3
  241.6 1.1 bitcast_add_fusion.1
  243.6 1.2 collective-permute-start.4
  245.0 5.0 %collective-permute-done.4 = bf16[2,64,768]{2,1,0:T(8,128)(2,1)S(1)} collective-permute-done((bf16[2,64,768]{2,1,0:T(8,128)(2,1)S(1)}, bf16[2,64,768]{2,1,0:T(8,128)(2,1)S(1)}, u32[]{:S(2)}, u32[]{:S(2)}) %collective-permute-start.4) | collective-permute-done | bytes 196640 | tf_op jit(solution)/shard_map/ppermute | solution.py:38
  250.0 2.7 multiply_reduce_fusion.3
  252.8 9.3 %all_gather.23 = bf16[2,256,768]{2,1,0:T(8,128)(2,1)S(1)} all-gather(bf16[2,64,768]{2,1,0:T(8,128)(2,1)S(1)} %fusion.38), channel_id=1, replica_groups=mesh['y'=4,'z'=4,'xh'=2,'xl'=2,'c'=2] {'xl','c'}, dimensions={1}, use_global_device_ids=true | all-gather | bytes 983040 | tf_op jit(solution)/shard_map/all_gather | solution.py:72
  262.2 1.4 convert_multiply_fusion
  263.7 1.4 broadcast_in_dim.50
  265.2 4.5 all-to-all-start.5
  270.5 3.0 convolution_convert_fusion
  273.5 3.5 reshape.617
  276.9 1.4 copy.95
  278.4 3.1 reshape.618
  281.4 3.3 convolution_convert_fusion.1
  284.8 1.8 convolution_convert_fusion.2
  287.0 3.2 fusion.1
  290.2 5.1 %all-to-all-done.5.g_ref = bf16[8,2,224,256]{3,2,1,0:T(8,128)(2,1)} async-done(((bf16[8,2,224,256]{3,2,1,0:T(8,128)(2,1)}), bf16[8,2,224,256]{3,2,1,0:T(8,128)(2,1)}, u32[]{:S(2)}, u32[]{:S(2)}) %all-to-all-start.5) | async-done | bytes 1835040 | tf_op jit(solution)/shard_map/all_to_all | solution.py:30
  295.3 4.9 %all-to-all-start.6 = ((bf16[32,80,768]{2,1,0:T(8,128)(2,1)}), bf16[32,80,768]{2,1,0:T(8,128)(2,1)}, u32[]{:S(2)}, u32[]{:S(2)}) async-start(bf16[32,80,768]{2,1,0:T(8,128)(2,1)} %fusion.1), calls=%async_computation.6 | async-start | bytes 7864320 | tf_op jit(solution)/shard_map/all_to_all | solution.py:30
  300.2 33.0 %shard_map.153 = (bf16[8,2,192,256]{3,2,1,0:T(8,128)(2,1)}, bf16[4,2,384,256]{3,2,1,0:T(8,128)(2,1)}) custom-call(s32[2]{0:T(128)} %lens_ref.3, s32[4]{0:T(128)} %add_multiply_fusion.start_ref, bf16[8,2,192,256]{3,2,1,0:T(8,128)(2,1)} %all-to-all-done.2.q_ref, bf16[4,2,384,256]{3,2,1,0:T(8,128)(2,1)} %copy-done.13, bf16[8,2,224,256]{3,2,1,0:T(8,128)(2,1)} %all-to-all-done.5.g_ref), custom_call_target="tpu_custom_call" | custom-call | flops 46000001024 | bytes 8000000 | tf_op jit(solution)/shard_map/pallas_call | solution.py:225
  333.1 21.1 %all-to-all-done.6 = bf16[32,80,768]{2,1,0:T(8,128)(2,1)} async-done(((bf16[32,80,768]{2,1,0:T(8,128)(2,1)}), bf16[32,80,768]{2,1,0:T(8,128)(2,1)}, u32[]{:S(2)}, u32[]{:S(2)}) %all-to-all-start.6) | async-done | bytes 3932192 | tf_op jit(solution)/shard_map/all_to_all | solution.py:30
  354.3 21.9 %all_to_all.55 = bf16[4,2,384,256]{3,2,1,0:T(8,128)(2,1)S(1)} all-to-all(bf16[4,2,384,256]{3,2,1,0:T(8,128)(2,1)} %get-tuple-element.20), channel_id=1, replica_groups=mesh['y'=4,'z'=4,'xh'=2,'xl'=2,'c'=2] {'y'}, dimensions={0} | all-to-all | bytes 3145728 | tf_op jit(solution)/shard_map/all_to_all | solution.py:30
  376.2 4.9 %all-to-all-start.7 = ((bf16[8,2,192,256]{3,2,1,0:T(8,128)(2,1)}), bf16[8,2,192,256]{3,2,1,0:T(8,128)(2,1)}, u32[]{:S(2)}, u32[]{:S(2)}) async-start(bf16[8,2,192,256]{3,2,1,0:T(8,128)(2,1)} %get-tuple-element.19), calls=%async_computation.7 | async-start | bytes 3145728 | tf_op jit(solution)/shard_map/all_to_all | solution.py:30
  382.3 2.4 fusion.5
  385.0 16.2 %all-to-all-done.7 = bf16[8,2,192,256]{3,2,1,0:T(8,128)(2,1)} async-done(((bf16[8,2,192,256]{3,2,1,0:T(8,128)(2,1)}), bf16[8,2,192,256]{3,2,1,0:T(8,128)(2,1)}, u32[]{:S(2)}, u32[]{:S(2)}) %all-to-all-start.7) | async-done | bytes 1572896 | tf_op jit(solution)/shard_map/all_to_all | solution.py:30
  401.2 1.7 convert_reduce_fusion.2
  404.1 1.5 copy.109
  405.6 6.1 %all-to-all-start.9 = ((bf16[32,24,768]{2,1,0:T(8,128)(2,1)}), bf16[32,24,768]{2,1,0:T(8,128)(2,1)}, u32[]{:S(2)}, u32[]{:S(2)}) async-start(bf16[32,24,768]{2,1,0:T(8,128)(2,1)} %bitcast.60), calls=%async_computation.9 | async-start | bytes 2359296 | tf_op jit(solution)/shard_map/all_to_all | solution.py:30
  412.9 1.2 copy-done.2
  414.1 2.8 collective-permute-start.5
  416.9 2.7 convert_reduce_fusion
  419.8 3.3 collective-permute-start.7
  424.4 1.9 collective-permute-done.7
  427.1 7.5 %collective-permute-start.6 = (bf16[2,64,768]{2,1,0:T(8,128)(2,1)S(1)}, bf16[2,64,768]{2,1,0:T(8,128)(2,1)S(1)}, u32[]{:S(2)}, u32[]{:S(2)}) collective-permute-start(bf16[2,64,768]{2,1,0:T(8,128)(2,1)S(1)} %fusion.32), channel_id=1, source_target_pairs={{0,2},{2,0},{1,3},{3,1},{4,6},{6,4},{5,7},{7,5},{8,10},{10,8},{9,1... | collective-permute-start | bytes 589832 | tf_op jit(solution)/shard_map/ppermute | solution.py:38
  434.6 1.4 convert_reduce_fusion.3
  438.3 5.7 %all-to-all-start.10 = ((bf16[4,32,192]{2,1,0:T(8,128)(2,1)}), bf16[4,32,192]{2,1,0:T(8,128)(2,1)S(1)}, u32[]{:S(2)}, u32[]{:S(2)}) async-start(bf16[4,32,192]{2,1,0:T(8,128)(2,1)} %copy.110), calls=%async_computation.10 | async-start | bytes 131072 | tf_op jit(solution)/shard_map/all_to_all | solution.py:30
  445.6 1.7 all-to-all-done.10
  (261 shorter events, 40.7 us)
Async XLA Ops:
  10.1 10.4 %all-to-all-start = ((bf16[4,56,192]{2,1,0:T(8,128)(2,1)}), bf16[4,56,192]{2,1,0:T(8,128)(2,1)S(1)}, u32[]{:S(2)}, u32[]{:S(2)}) async-start(bf16[4,56,192]{2,1,0:T(8,128)(2,1)} %pad_maximum_fusion.7), calls=%async_computation | async-start | bytes 229376 | tf_op jit(solution)/shard_map/all_to_all | solution.py:30
  14.8 173.8 %all-gather.3.cloned.1.call-start = ((), (), s32[]{:S(2)}) async-start(), calls=%async_computation.11 | async-start | bytes 5271552 | tf_op jit(solution)/shard_map/all_gather | solution.py:276
  14.8 5.6 %collective-permute-start = (bf16[96,192]{1,0:T(8,128)(2,1)}, bf16[96,192]{1,0:T(8,128)(2,1)S(1)}, u32[]{:S(2)}, u32[]{:S(2)}) collective-permute-start(bf16[96,192]{1,0:T(8,128)(2,1)} %param.15), channel_id=1, source_target_pairs={{0,0},{1,32},{2,64},{3,96},{32,1},{33,33},{34,65},{35,97},{64,2},{... | collective-permute-start | bytes 110600 | tf_op jit(solution)/shard_map/ppermute | solution.py:270
  22.3 14.1 %copy-start.25 = (bf16[2,64,768]{2,1,0:T(8,128)(2,1)S(1)}, bf16[2,64,768]{2,1,0:T(8,128)(2,1)}, u32[]{:S(2)}) copy-start(bf16[2,64,768]{2,1,0:T(8,128)(2,1)} %param.9) | copy-start | bytes 589828
  23.5 31.3 %all-to-all-start.1 = ((bf16[32,24,576]{2,1,0:T(8,128)(2,1)}), bf16[32,24,576]{2,1,0:T(8,128)(2,1)S(1)}, u32[]{:S(2)}, u32[]{:S(2)}) async-start(bf16[32,24,576]{2,1,0:T(8,128)(2,1)} %broadcast_in_dim.47), calls=%async_computation.1 | async-start | bytes 1966080 | tf_op jit(solution)/shard_map/all_to_all | solution.py:30
  36.4 19.4 %copy-start.27 = (f32[32,256]{1,0:T(8,128)}, f32[32,256]{1,0:T(8,128)S(1)}, u32[]{:S(2)}) copy-start(f32[32,256]{1,0:T(8,128)S(1)} %get-tuple-element.72) | copy-start | bytes 98308
  36.4 19.4 %copy-start.29 = (f32[32,256]{1,0:T(8,128)}, f32[32,256]{1,0:T(8,128)S(1)}, u32[]{:S(2)}) copy-start(f32[32,256]{1,0:T(8,128)S(1)} %get-tuple-element.73) | copy-start | bytes 98308
  57.3 25.6 %all-to-all-start.3 = ((bf16[4,2,384,256]{3,2,1,0:T(8,128)(2,1)}), bf16[4,2,384,256]{3,2,1,0:T(8,128)(2,1)S(1)}, u32[]{:S(2)}, u32[]{:S(2)}) async-start(bf16[4,2,384,256]{3,2,1,0:T(8,128)(2,1)} %broadcast_in_dim.49), calls=%async_computation.3 | async-start | bytes 3145728 | tf_op jit(solution)/shard_map/all_to_all | solution.py:30
  82.8 1.7 copy-start.13
  84.6 47.2 %all-to-all-start.2 = ((bf16[8,2,192,256]{3,2,1,0:T(8,128)(2,1)}), bf16[8,2,192,256]{3,2,1,0:T(8,128)(2,1)}, u32[]{:S(2)}, u32[]{:S(2)}) async-start(bf16[8,2,192,256]{3,2,1,0:T(8,128)(2,1)} %broadcast_in_dim.48), calls=%async_computation.2 | async-start | bytes 3145728 | tf_op jit(solution)/shard_map/all_to_all | solution.py:30
  148.5 3.8 copy-start.47
  148.5 25.6 %all-to-all-start.4 = ((bf16[8,2,208,256]{3,2,1,0:T(8,128)(2,1)}), bf16[8,2,208,256]{3,2,1,0:T(8,128)(2,1)S(1)}, u32[]{:S(2)}, u32[]{:S(2)}) async-start(bf16[8,2,208,256]{3,2,1,0:T(8,128)(2,1)} %shard_map.152), calls=%async_computation.4 | async-start | bytes 3407872 | tf_op jit(solution)/shard_map/all_to_all | solution.py:30
  188.6 13.5 %copy-start.10 = (bf16[2,768,256]{2,1,0:T(8,128)(2,1)}, bf16[2,768,256]{2,1,0:T(8,128)(2,1)S(1)}, u32[]{:S(2)}) copy-start(bf16[2,768,256]{2,1,0:T(8,128)(2,1)S(1)} %all_gather.19) | copy-start | bytes 2359300
  204.7 1.3 copy-start.14
  205.1 1.7 copy-start.21
  206.0 1.3 copy-start.4
  206.8 2.5 copy-start.49
  207.3 2.9 copy-start.18
  210.1 2.1 copy-start.26
  212.1 4.8 %collective-permute-start.1 = (bf16[2,2,64,768]{3,2,0,1:T(8,128)(2,1)S(1)}, bf16[2,2,64,768]{3,2,0,1:T(8,128)(2,1)S(1)}, u32[]{:S(2)}, u32[]{:S(2)}) collective-permute-start(bf16[2,2,64,768]{3,2,0,1:T(8,128)(2,1)S(1)} %fusion.13), channel_id=1, source_target_pairs={{0,1},{1,0},{2,3},{3,2},{4,5},{5,4},{6,7},{7,6},{8,9},{9,8},{10,11... | collective-permute-start | bytes 1179656 | tf_op jit(solution)/shard_map/ppermute | solution.py:38
  218.1 6.7 %copy-start.12 = (bf16[2,64,768]{2,1,0:T(8,128)(2,1)S(1)}, bf16[2,64,768]{2,1,0:T(8,128)(2,1)}, u32[]{:S(2)}) copy-start(bf16[2,64,768]{2,1,0:T(8,128)(2,1)} %param.17) | copy-start | bytes 589828
  218.1 6.7 %copy-start.37 = (f32[2,64]{1,0:T(2,128)S(1)}, f32[2,64]{1,0:T(2,128)}, u32[]{:S(2)}) copy-start(f32[2,64]{1,0:T(2,128)} %compare_convert_fusion) | copy-start | bytes 1540
  218.1 16.7 %copy-start.53 = (f32[512,768]{1,0:T(8,128)S(1)}, f32[512,768]{1,0:T(8,128)}, u32[]{:S(2)}) copy-start(f32[512,768]{1,0:T(8,128)} %get-tuple-element.77) | copy-start | bytes 4718596
  218.1 6.2 %collective-permute-start.2 = (bf16[2,64,768]{2,1,0:T(8,128)(2,1)S(1)}, bf16[2,64,768]{2,1,0:T(8,128)(2,1)S(1)}, u32[]{:S(2)}, u32[]{:S(2)}) collective-permute-start(bf16[2,64,768]{2,1,0:T(8,128)(2,1)S(1)} %fusion.30), channel_id=1, source_target_pairs={{0,2},{2,0},{1,3},{3,1},{4,6},{6,4},{5,7},{7,5},{8,10},{10,8},{9,1... | collective-permute-start | bytes 589832 | tf_op jit(solution)/shard_map/ppermute | solution.py:38
  218.3 34.4 %copy-start.35 = (f32[2,64]{1,0:T(2,128)}, f32[2,64]{1,0:T(2,128)S(1)}, u32[]{:S(2)}) copy-start(f32[2,64]{1,0:T(2,128)S(1)} %add_rsqrt_fusion.2) | copy-start | bytes 1540
  224.6 10.2 %copy-start.17 = (bf16[768,768]{1,0:T(8,128)(2,1)S(1)}, bf16[768,768]{1,0:T(8,128)(2,1)}, u32[]{:S(2)}) copy-start(bf16[768,768]{1,0:T(8,128)(2,1)} %reshape.613) | copy-start | bytes 3538948
  224.6 10.2 %copy-start.50 = (f32[512,768]{1,0:T(8,128)S(1)}, f32[512,768]{1,0:T(8,128)}, u32[]{:S(2)}) copy-start(f32[512,768]{1,0:T(8,128)} %copy-done.49) | copy-start | bytes 4718596
  234.8 1.2 copy-start.23
  234.8 1.6 copy-start.15
  236.3 1.5 copy-start.5
  238.7 6.1 %copy-start.33 = (f32[2,3,256]{2,1,0:T(4,128)S(1)}, f32[2,3,256]{2,1,0:T(4,128)}, u32[]{:S(2)}) copy-start(f32[2,3,256]{2,1,0:T(4,128)} %get-tuple-element.34) | copy-start | bytes 18436
  238.7 6.2 %copy-start.32 = (f32[32,24]{1,0:T(8,128)S(1)}, f32[32,24]{1,0:T(8,128)}, u32[]{:S(2)}) copy-start(f32[32,24]{1,0:T(8,128)} %get-tuple-element.31) | copy-start | bytes 9220
  239.5 2.1 collective-permute-start.3
  243.6 6.4 %collective-permute-start.4 = (bf16[2,64,768]{2,1,0:T(8,128)(2,1)S(1)}, bf16[2,64,768]{2,1,0:T(8,128)(2,1)S(1)}, u32[]{:S(2)}, u32[]{:S(2)}) collective-permute-start(bf16[2,64,768]{2,1,0:T(8,128)(2,1)S(1)} %fusion.31), channel_id=1, source_target_pairs={{0,2},{2,0},{1,3},{3,1},{4,6},{6,4},{5,7},{7,5},{8,10},{10,8},{9,1... | collective-permute-start | bytes 589832 | tf_op jit(solution)/shard_map/ppermute | solution.py:38
  245.0 17.2 %copy-start.7 = (f32[2,192,256]{2,1,0:T(8,128)S(1)}, f32[2,192,256]{2,1,0:T(8,128)}, u32[]{:S(2)}) copy-start(f32[2,192,256]{2,1,0:T(8,128)} %copy-done.6) | copy-start | bytes 1179652
  252.6 10.9 %copy-start.8 = (f32[2,64,768]{2,1,0:T(8,128)}, f32[2,64,768]{2,1,0:T(8,128)S(1)}, u32[]{:S(2)}) copy-start(f32[2,64,768]{2,1,0:T(8,128)S(1)} %get-tuple-element.36) | copy-start | bytes 1179652
  252.6 10.9 %copy-start.38 = (f32[2,64]{1,0:T(2,128)}, f32[2,64]{1,0:T(2,128)S(1)}, u32[]{:S(2)}) copy-start(f32[2,64]{1,0:T(2,128)S(1)} %broadcast_multiply_fusion.1) | copy-start | bytes 1540
  252.7 10.9 %copy-start.40 = (f32[2,64]{1,0:T(2,128)}, f32[2,64]{1,0:T(2,128)S(1)}, u32[]{:S(2)}) copy-start(f32[2,64]{1,0:T(2,128)S(1)} %broadcast_multiply_fusion.2) | copy-start | bytes 1540
  265.2 4.5 copy-start.43
  265.2 4.6 %copy-start.42 = (bf16[768]{0:T(1024)(128)(2,1)S(1)}, bf16[768]{0:T(1024)(128)(2,1)}, u32[]{:S(2)}) copy-start(bf16[768]{0:T(1024)(128)(2,1)} %get-tuple-element.29) | copy-start | bytes 4612
  265.2 5.3 %copy-start.24 = (bf16[2,256,768]{2,1,0:T(8,128)(2,1)S(1)}, bf16[2,256,768]{2,1,0:T(8,128)(2,1)}, u32[]{:S(2)}) copy-start(bf16[2,256,768]{2,1,0:T(8,128)(2,1)} %copy-done.23) | copy-start | bytes 2359300
  265.2 30.1 %all-to-all-start.5 = ((bf16[8,2,224,256]{3,2,1,0:T(8,128)(2,1)}), bf16[8,2,224,256]{3,2,1,0:T(8,128)(2,1)}, u32[]{:S(2)}, u32[]{:S(2)}) async-start(bf16[8,2,224,256]{3,2,1,0:T(8,128)(2,1)} %broadcast_in_dim.50), calls=%async_computation.5 | async-start | bytes 3670016 | tf_op jit(solution)/shard_map/all_to_all | solution.py:30
  281.4 3.4 copy-start.22
  281.4 3.3 copy-start.52
  284.8 1.9 copy-start.45
  284.8 1.9 copy-start.44
  284.8 2.0 copy-start.34
  295.3 59.0 %all-to-all-start.6 = ((bf16[32,80,768]{2,1,0:T(8,128)(2,1)}), bf16[32,80,768]{2,1,0:T(8,128)(2,1)}, u32[]{:S(2)}, u32[]{:S(2)}) async-start(bf16[32,80,768]{2,1,0:T(8,128)(2,1)} %fusion.1), calls=%async_computation.6 | async-start | bytes 7864320 | tf_op jit(solution)/shard_map/all_to_all | solution.py:30
  376.2 25.0 %all-to-all-start.7 = ((bf16[8,2,192,256]{3,2,1,0:T(8,128)(2,1)}), bf16[8,2,192,256]{3,2,1,0:T(8,128)(2,1)}, u32[]{:S(2)}, u32[]{:S(2)}) async-start(bf16[8,2,192,256]{3,2,1,0:T(8,128)(2,1)} %get-tuple-element.19), calls=%async_computation.7 | async-start | bytes 3145728 | tf_op jit(solution)/shard_map/all_to_all | solution.py:30
  385.0 17.9 %copy-start.28 = (f32[32,256]{1,0:T(8,128)S(1)}, f32[32,256]{1,0:T(8,128)}, u32[]{:S(2)}) copy-start(f32[32,256]{1,0:T(8,128)} %copy-done.27) | copy-start | bytes 98308
  385.0 17.9 %copy-start.30 = (f32[32,256]{1,0:T(8,128)S(1)}, f32[32,256]{1,0:T(8,128)}, u32[]{:S(2)}) copy-start(f32[32,256]{1,0:T(8,128)} %copy-done.29) | copy-start | bytes 98308
  405.6 6.4 %copy-start.1 = (bf16[32,24,576]{2,1,0:T(8,128)(2,1)S(1)}, bf16[32,24,576]{2,1,0:T(8,128)(2,1)}, u32[]{:S(2)}) copy-start(bf16[32,24,576]{2,1,0:T(8,128)(2,1)} %copy-done) | copy-start | bytes 2654212
  405.6 29.0 %all-to-all-start.9 = ((bf16[32,24,768]{2,1,0:T(8,128)(2,1)}), bf16[32,24,768]{2,1,0:T(8,128)(2,1)}, u32[]{:S(2)}, u32[]{:S(2)}) async-start(bf16[32,24,768]{2,1,0:T(8,128)(2,1)} %bitcast.60), calls=%async_computation.9 | async-start | bytes 2359296 | tf_op jit(solution)/shard_map/all_to_all | solution.py:30
  412.9 1.2 copy-start.2
  414.1 12.9 %copy-start.3 = (f32[2,2,2,64,768]{4,3,2,1,0:T(8,128)S(1)}, f32[2,2,2,64,768]{4,3,2,1,0:T(8,128)}, u32[]{:S(2)}) copy-start(f32[2,2,2,64,768]{4,3,2,1,0:T(8,128)} %copy-done.2) | copy-start | bytes 4718596
  414.1 12.9 %collective-permute-start.5 = (bf16[2,2,64,768]{3,2,0,1:T(8,128)(2,1)S(1)}, bf16[2,2,64,768]{3,2,0,1:T(8,128)(2,1)S(1)}, u32[]{:S(2)}, u32[]{:S(2)}) collective-permute-start(bf16[2,2,64,768]{3,2,0,1:T(8,128)(2,1)S(1)} %fusion.15), channel_id=1, source_target_pairs={{0,1},{1,0},{2,3},{3,2},{4,5},{5,4},{6,7},{7,6},{8,9},{9,8},{10,11... | collective-permute-start | bytes 1179656 | tf_op jit(solution)/shard_map/ppermute | solution.py:38
  419.8 6.5 %collective-permute-start.7 = (bf16[96,192]{1,0:T(8,128)(2,1)S(1)}, bf16[96,192]{1,0:T(8,128)(2,1)S(1)}, u32[]{:S(2)}, u32[]{:S(2)}) collective-permute-start(bf16[96,192]{1,0:T(8,128)(2,1)S(1)} %convert_element_type.250), channel_id=1, source_target_pairs={{0,0},{1,32},{2,64},{3,96},{32,1},{33,33},{34,65},{35,97},{64,2},{... | collective-permute-start | bytes 110600 | tf_op jit(solution)/shard_map/ppermute | solution.py:407
  427.0 17.0 %copy-start.9 = (f32[2,64,768]{2,1,0:T(8,128)S(1)}, f32[2,64,768]{2,1,0:T(8,128)}, u32[]{:S(2)}) copy-start(f32[2,64,768]{2,1,0:T(8,128)} %copy-done.8) | copy-start | bytes 1179652
  427.0 17.0 %copy-start.36 = (f32[2,64]{1,0:T(2,128)S(1)}, f32[2,64]{1,0:T(2,128)}, u32[]{:S(2)}) copy-start(f32[2,64]{1,0:T(2,128)} %copy-done.35) | copy-start | bytes 1540
  427.1 17.0 %copy-start.39 = (f32[2,64]{1,0:T(2,128)S(1)}, f32[2,64]{1,0:T(2,128)}, u32[]{:S(2)}) copy-start(f32[2,64]{1,0:T(2,128)} %copy-done.38) | copy-start | bytes 1540
  427.1 17.0 %copy-start.41 = (f32[2,64]{1,0:T(2,128)S(1)}, f32[2,64]{1,0:T(2,128)}, u32[]{:S(2)}) copy-start(f32[2,64]{1,0:T(2,128)} %copy-done.40) | copy-start | bytes 1540
  427.1 16.9 %collective-permute-start.6 = (bf16[2,64,768]{2,1,0:T(8,128)(2,1)S(1)}, bf16[2,64,768]{2,1,0:T(8,128)(2,1)S(1)}, u32[]{:S(2)}, u32[]{:S(2)}) collective-permute-start(bf16[2,64,768]{2,1,0:T(8,128)(2,1)S(1)} %fusion.32), channel_id=1, source_target_pairs={{0,2},{2,0},{1,3},{3,1},{4,6},{6,4},{5,7},{7,5},{8,10},{10,8},{9,1... | collective-permute-start | bytes 589832 | tf_op jit(solution)/shard_map/ppermute | solution.py:38
  436.0 11.8 %copy-start.46 = (pred[3]{0:T(512)(128)(4,1)S(1)}, pred[3]{0:T(512)(128)(4,1)}, u32[]{:S(2)}) copy-start(pred[3]{0:T(512)(128)(4,1)} %compare_and_fusion) | copy-start | bytes 13
  438.3 8.9 %all-to-all-start.10 = ((bf16[4,32,192]{2,1,0:T(8,128)(2,1)}), bf16[4,32,192]{2,1,0:T(8,128)(2,1)S(1)}, u32[]{:S(2)}, u32[]{:S(2)}) async-start(bf16[4,32,192]{2,1,0:T(8,128)(2,1)} %copy.110), calls=%async_computation.10 | async-start | bytes 131072 | tf_op jit(solution)/shard_map/all_to_all | solution.py:30
  (9 other events, 8.6 us)
Sparse Core Ops, SparseCore 0:
  21.7 118.6 all-gather.2
